TPU v7x, 128 devices: a whole 4x4x4 slice. The times are simulated.
128 devices in a mesh: span: 8 (over x, core), cnn: 16 (over z, y).
Axes of the slice: x: 4, y: 4, z: 4, core: 2. Of those that a mesh axis runs over, the one named last changes fastest.
Arguments:
- views: bfloat16 [1024, 4, 4, 128, 256], P(('span', 'cnn')), may hold values from -11 to 11
- live_counts: int32 [8, 16], P('span', 'cnn'), may hold values from 1 to 8, 32 in all within a row
- skeleton_edges: int32 [1024, 4], P(('span', 'cnn')), may hold values from 0 to 11
- boundary_rows: int32 [256], P(('span', 'cnn')), may hold values from 0 to 7
- patch_weight: bfloat16 [4, 4, 4, 128], replicated, may hold values from -1 to 1
- conv_first: bfloat16 [3, 3, 128, 128], replicated, may hold values from -0.25 to 0.25
- conv_second: bfloat16 [3, 3, 128, 128], replicated, may hold values from -0.25 to 0.25
- conv_third: bfloat16 [3, 3, 128, 256], replicated, may hold values from -0.25 to 0.25
- conv_fourth: bfloat16 [3, 3, 256, 256], replicated, may hold values from -0.1875 to 0.1875
- head_weight: float32 [256, 7], replicated, may hold values from -1.5 to 1.5
Outputs:
- labels: float32 [1024, 7], P(('span', 'cnn'))
Inputs may be any that keep to these rules, and one draw needn't show every extreme that they name: `live_counts`: in each span the 16 counts sum to 32 and the largest is exactly 8. `skeleton_edges`: an entry below 4 names an exported row of a neighbouring span, any other a location of the own device.
All inputs are finite; a program needn't handle non-finite values. No bound on the sum of `live_counts` on one device may be relied on, other than what follows from the above.
Results may differ from a plain program's by a relative error of at most 0.0004.
Values may be sent and summed in bfloat16 or wider, within the bound.
A program may use at most 128 MiB of HBM per device.

v0:
```python
import jax
import jax.numpy as jnp
from jax import lax
from jax.sharding import PartitionSpec as P

VIEWS = 4
PATCH = 4
BAL = 2
ITERS = 2


LAMBDA_MIX = 0.5
TILE_LAYOUT = ("NCHW", "HWIO", "NHWC")
CONV_LAYOUT = ("NHWC", "HWIO", "NHWC")


def with_halo(block, sides, width):
    for axis, dim in sides:
        count = lax.axis_size(axis)
        forward = [(i, i + 1) for i in range(count - 1)]
        backward = [(target, source) for source, target in forward]
        low = lax.ppermute(
            lax.slice_in_dim(block, block.shape[dim] - width, None, axis=dim), axis, forward
        )
        high = lax.ppermute(lax.slice_in_dim(block, 0, width, axis=dim), axis, backward)
        block = jnp.concatenate([low, block, high], axis=dim)
    return block


def convolve(inputs, kernel, strides, padding_mode, layout):
    return lax.conv_general_dilated(
        inputs,
        kernel,
        strides,
        padding_mode,
        dimension_numbers=layout,
        preferred_element_type=jnp.float32,
    )


def network(batch, weights):
    embedded = convolve(batch, weights[0], (PATCH, PATCH), "VALID", TILE_LAYOUT)
    first_map = jax.nn.relu(embedded).astype(jnp.bfloat16)
    raised = jax.nn.relu(convolve(first_map, weights[1], (1, 1), "SAME", CONV_LAYOUT))
    batch_size, map_rows, map_cols, channels = raised.shape
    pooled = (
        raised.reshape(batch_size, map_rows // 2, 2, map_cols // 2, 2, channels)
        .mean(axis=(2, 4))
        .astype(jnp.bfloat16)
    )
    third_map = jax.nn.relu(convolve(pooled, weights[2], (1, 1), "SAME", CONV_LAYOUT)).astype(
        jnp.bfloat16
    )
    fourth_map = jax.nn.relu(convolve(third_map, weights[3], (1, 1), "SAME", CONV_LAYOUT)).astype(
        jnp.bfloat16
    )
    fifth_map = jax.nn.relu(convolve(fourth_map, weights[4], (1, 1), "SAME", CONV_LAYOUT))
    feature = jnp.mean(fifth_map, axis=(1, 2))
    return jnp.dot(
        feature, weights[5], preferred_element_type=jnp.float32, precision=lax.Precision.HIGHEST
    )


def send_order(units, first_rank, peer_count):
    unit_total = units.shape[0]
    rounds = -(-unit_total // peer_count)
    padding = [(0, rounds * peer_count - unit_total)] + [(0, 0)] * (units.ndim - 1)
    shaped = jnp.pad(units, padding).reshape((rounds, peer_count) + units.shape[1:])
    return jnp.roll(shaped, first_rank, axis=1)


def restore_order(returned, first_rank, unit_total):
    rounds = returned.shape[0]
    peer_count = returned.shape[1]
    settled = jnp.roll(returned, -first_rank, axis=1)
    return settled.reshape((rounds * peer_count,) + returned.shape[2:])[:unit_total]


def arrival_plan(unit_counts, first_ranks, position, rounds, wanted):
    peer_count = unit_counts.shape[0]
    block_index = jnp.arange(rounds, dtype=jnp.int32)[:, None]
    slot_unit = (position - first_ranks[None, :]) % peer_count + block_index * peer_count
    alive_slot = (slot_unit < unit_counts[None, :]).reshape(-1)
    target = ((first_ranks[None, :] + slot_unit - position) // peer_count).reshape(-1)
    wanted_rows = jnp.arange(wanted, dtype=jnp.int32)[:, None]
    matches = alive_slot[None, :] & (target[None, :] == wanted_rows)
    slot_ids = jnp.arange(rounds * peer_count, dtype=jnp.int32)[None, :]
    chosen = jnp.sum(jnp.where(matches, slot_ids, 0), axis=1)
    return (chosen, alive_slot.astype(jnp.float32), jnp.clip(target, 0, wanted - 1))


def per_device(
    views,
    live_counts,
    skeleton_edges,
    boundary_rows,
    patch_weight,
    conv_first,
    conv_second,
    conv_third,
    conv_fourth,
    head_weight,
):
    weights = (patch_weight, conv_first, conv_second, conv_third, conv_fourth, head_weight)
    location_total = views.shape[0]
    own_count = live_counts[0, 0]
    view_shape = views.shape[2:]
    peer_count = lax.axis_size("cnn")
    position = lax.axis_index("cnn")
    all_counts = lax.all_gather(live_counts, "cnn", axis=1, tiled=True).reshape(peer_count)
    first_ranks = jnp.cumsum(all_counts) - all_counts
    first_rank = first_ranks[position]
    outgoing = send_order(views, first_rank, peer_count)
    rounds = outgoing.shape[0]
    incoming = lax.all_to_all(outgoing, "cnn", split_axis=1, concat_axis=1, tiled=True)
    chosen, alive_slot, target = arrival_plan(all_counts, first_ranks, position, rounds, BAL)
    gathered = incoming.reshape((rounds * peer_count,) + views.shape[1:])[chosen]
    labelled = network(gathered.reshape((BAL * VIEWS,) + view_shape), weights).reshape(
        BAL, VIEWS, -1
    )
    answers = (labelled[target] * alive_slot[:, None, None]).reshape(
        (rounds, peer_count) + labelled.shape[1:]
    )
    returned = lax.all_to_all(answers, "cnn", split_axis=1, concat_axis=1, tiled=True)
    view_logits = restore_order(returned, first_rank, location_total)
    alive_mask = (jnp.arange(location_total, dtype=jnp.int32) < own_count).astype(jnp.float32)[
        :, None
    ]
    smooth = jnp.mean(view_logits, axis=1) * alive_mask
    rim_rows = boundary_rows.shape[0]
    exported_ids = boundary_rows % own_count
    border = 2 * rim_rows
    lookup = jnp.where(
        skeleton_edges < border, skeleton_edges, border + (skeleton_edges - border) % own_count
    )
    for iteration in range(ITERS):
        exported = smooth[exported_ids]
        bordered = with_halo(exported, (("span", 0),), rim_rows)
        row_table = jnp.concatenate([bordered[:rim_rows], bordered[2 * rim_rows :], smooth], axis=0)
        neighbours = row_table[lookup]
        smooth = (
            (1.0 - LAMBDA_MIX) * smooth + LAMBDA_MIX * jnp.mean(neighbours, axis=1)
        ) * alive_mask
    return smooth


def solution(mesh):
    placed = (
        P(("span", "cnn"), None, None, None, None),
        P("span", "cnn"),
        P(("span", "cnn"), None),
        P(("span", "cnn")),
        P(),
        P(),
        P(),
        P(),
        P(),
        P(),
    )
    return jax.shard_map(
        per_device, mesh=mesh, in_specs=placed, out_specs=P(("span", "cnn"), None), check_vma=False
    )
```

profile of v0, /device:TPU:1, one launch (start us, length us, event | category | flops | bytes accessed | tf_op | source)
XLA Modules:
  0.0 410.9 jit_solution(9836457212976298909)
XLA Ops:
  0.8 1.2 dynamic-slice
  2.0 0.7 bitcast_dynamic-update-slice_fusion
  2.7 14.8 %all-reduce.1 = s32[16]{0:T(128)S(1)} all-reduce(s32[16]{0:T(128)S(1)} %bitcast_dynamic-update-slice_fusion), channel_id=1, replica_groups=mesh['span'=8,'cnn'=16] {'cnn'}, use_global_device_ids=true, to_apply=%add.1 | all-reduce | flops 16 | bytes 128 | tf_op jit(solution)/shard_map/reshape | solution.py:110
  20.3 9.3 %pad_bitcast_fusion = bf16[1,16,4,4,128,256]{5,4,3,2,0,1:T(8,128)(2,1)} fusion(bf16[8,4,4,128,256]{4,3,2,1,0:T(8,128)(2,1)} %param.10), kind=kLoop, calls=%fused_computation.9 | loop fusion | bytes 25165824 | tf_op jit(solution)/shard_map/reshape | solution.py:68
  29.6 16.0 %fusion = bf16[1,16,4,4,128,256]{5,4,3,2,0,1:T(8,128)(2,1)} fusion(s32[]{:T(128)S(6)} %select_n.94, bf16[1,16,4,4,128,256]{5,4,3,2,0,1:T(8,128)(2,1)} %pad_bitcast_fusion), kind=kLoop, calls=%fused_computation.8 | loop fusion | flops 8388608 | bytes 33554436 | tf_op jit(solution)/shard_map/jit(_roll_dynamic)/concatenate | solution.py:69
  45.7 5.3 %all-to-all-start = ((bf16[1,16,4,4,128,256]{5,4,3,2,0,1:T(8,128)(2,1)}), bf16[1,16,4,4,128,256]{5,4,3,2,0,1:T(8,128)(2,1)}, u32[]{:S(2)}, u32[]{:S(2)}) async-start(bf16[1,16,4,4,128,256]{5,4,3,2,0,1:T(8,128)(2,1)} %fusion), calls=%async_computation | async-start | bytes 33554432 | tf_op jit(solution)/shard_map/all_to_all | solution.py:115
  51.6 237.7 %all-to-all-done = bf16[1,16,4,4,128,256]{5,4,3,2,0,1:T(8,128)(2,1)} async-done(((bf16[1,16,4,4,128,256]{5,4,3,2,0,1:T(8,128)(2,1)}), bf16[1,16,4,4,128,256]{5,4,3,2,0,1:T(8,128)(2,1)}, u32[]{:S(2)}, u32[]{:S(2)}) %all-to-all-start) | async-done | bytes 16777248 | tf_op jit(solution)/shard_map/all_to_all | solution.py:115
  289.4 6.4 %gather_fusion = bf16[2,4,4,128,256]{4,3,2,1,0:T(8,128)(2,1)S(1)} fusion(bf16[16,4,4,128,256]{4,3,2,1,0:T(8,128)(2,1)} %bitcast.5, s32[1024]{0:T(1024)S(1)} %pad_clamp_fusion.3), kind=kCustom, calls=%fused_computation | custom fusion | bytes 4194312 | tf_op jit(solution)/shard_map/gather | solution.py:117
  295.9 24.0 %copy.31 = bf16[8,4,128,256]{0,1,3,2:T(4,128)(2,1)} copy(bf16[8,4,128,256]{3,2,1,0:T(8,128)(2,1)S(1)} %bitcast.69) | data formatting | bytes 4194304 | tf_op jit(solution)/shard_map/reshape | solution.py:118
  319.8 18.9 %fusion.24 = bf16[8,32,64,128]{3,0,2,1:T(8,128)(2,1)S(1)} fusion(bf16[8,4,128,256]{0,1,3,2:T(4,128)(2,1)} %copy.31, bf16[4,4,4,128]{3,2,1,0:T(4,128)(2,1)S(1)} %copy-done.5), kind=kOutput, calls=%fused_computation.69 | convolution fusion | flops 268435456 | bytes 6307840 | tf_op jit(solution)/shard_map/conv_general_dilated | solution.py:31
  338.8 12.1 %fusion.2 = f32[8,32,64,128]{3,0,2,1:T(8,128)} fusion(bf16[3,3,128,128]{3,2,1,0:T(8,128)(2,1)S(1)} %copy-done.4, bf16[8,32,64,128]{3,0,2,1:T(8,128)(2,1)S(1)} %fusion.24), kind=kOutput, calls=%fused_computation.12 | convolution fusion | flops 4690280448 | bytes 12877824 | tf_op jit(solution)/shard_map/conv_general_dilated | solution.py:31
  350.9 4.3 %reduce_sum.58 = f32[8,16,32,128]{3,0,2,1:T(8,128)S(1)} reduce(f32[8,16,2,32,2,128]{5,0,4,3,2,1:T(8,128)} %bitcast.70, f32[]{:T(128)} %constant.110.clone.1), dimensions={2,4}, to_apply=%region_2.3 | reduce | flops 1572864 | bytes 10485764 | tf_op jit(solution)/shard_map/reduce_sum | solution.py:48
  355.2 13.3 %maximum_convert_fusion.4 = bf16[8,16,32,256]{3,0,2,1:T(8,128)(2,1)} fusion(bf16[3,3,128,256]{3,2,1,0:T(8,128)(2,1)} %param.17, bf16[3,3,128,128]{3,2,1,0:T(8,128)(2,1)} %param.16, f32[8,16,32,128]{3,0,2,1:T(8,128)S(1)} %reduce_sum.58), kind=kOutput, calls=%fused_computation.14 | convolution fusion | flops 3404726272 | bytes 5079040 | tf_op jit(solution)/shard_map/conv_general_dilated | solution.py:31
  368.5 6.9 %maximum_reduce_fusion = f32[8,256]{1,0:T(8,128)S(1)} fusion(bf16[8,16,32,256]{3,0,2,1:T(8,128)(2,1)} %maximum_convert_fusion.4, bf16[3,3,256,256]{3,2,1,0:T(8,128)(2,1)S(1)} %copy-done), kind=kOutput, calls=%fused_computation.13 | convolution fusion | flops 4536137728 | bytes 3284992 | tf_op jit(solution)/shard_map/conv_general_dilated | solution.py:31
  376.2 0.7 fusion.5
  376.9 4.9 %all-to-all-start.1 = ((f32[1,16,4,7]{3,2,0,1:T(4,128)}), f32[1,16,4,7]{3,2,0,1:T(4,128)S(1)}, u32[]{:S(2)}, u32[]{:S(2)}) async-start(f32[1,16,4,7]{3,2,0,1:T(4,128)} %fusion.5), calls=%async_computation.1 | async-start | bytes 65536 | tf_op jit(solution)/shard_map/all_to_all | solution.py:124
  382.5 5.8 %all-to-all-done.1 = f32[1,16,4,7]{3,2,0,1:T(4,128)S(1)} async-done(((f32[1,16,4,7]{3,2,0,1:T(4,128)}), f32[1,16,4,7]{3,2,0,1:T(4,128)S(1)}, u32[]{:S(2)}, u32[]{:S(2)}) %all-to-all-start.1) | async-done | bytes 1824 | tf_op jit(solution)/shard_map/all_to_all | solution.py:124
  389.2 8.6 %collective-permute-start.1 = (f32[2,7]{1,0:T(2,128)S(1)}, f32[2,7]{1,0:T(2,128)S(1)}, u32[]{:S(2)}, u32[]{:S(2)}) collective-permute-start(f32[2,7]{1,0:T(2,128)S(1)} %gather_fusion.2), channel_id=1, source_target_pairs={{16,0},{32,16},{48,32},{64,48},{80,64},{96,80},{112,96},{17,1},{33... | collective-permute-start | bytes 176 | tf_op jit(solution)/shard_map/ppermute | solution.py:25
  397.8 3.0 collective-permute-start
  400.9 0.7 collective-permute-done
  402.8 1.9 collective-permute-start.3
  404.7 4.2 %collective-permute-start.2 = (f32[2,7]{1,0:T(2,128)S(1)}, f32[2,7]{1,0:T(2,128)S(1)}, u32[]{:S(2)}, u32[]{:S(2)}) collective-permute-start(f32[2,7]{1,0:T(2,128)S(1)} %gather_fusion.4), channel_id=1, source_target_pairs={{0,16},{16,32},{32,48},{48,64},{64,80},{80,96},{96,112},{1,17},{17... | collective-permute-start | bytes 176 | tf_op jit(solution)/shard_map/ppermute | solution.py:22
  408.9 0.7 collective-permute-done.2
  410.2 0.7 add_multiply_fusion
  (49 shorter events, 5.0 us)
Async XLA Ops:
  0.0 368.5 %copy-start = (bf16[3,3,256,256]{3,2,1,0:T(8,128)(2,1)S(1)}, bf16[3,3,256,256]{3,2,1,0:T(8,128)(2,1)}, u32[]{:S(2)}) copy-start(bf16[3,3,256,256]{3,2,1,0:T(8,128)(2,1)} %param.18) | copy-start | bytes 3538948
  45.7 5.3 %copy-start.2 = (s32[8,4]{0,1:T(4,128)S(1)}, s32[8,4]{0,1:T(4,128)}, u32[]{:S(2)}) copy-start(s32[8,4]{0,1:T(4,128)} %param.12) | copy-start | bytes 388
  45.7 5.8 %copy-start.3 = (s32[2]{0:T(128)S(1)}, s32[2]{0:T(128)}, u32[]{:S(2)}) copy-start(s32[2]{0:T(128)} %param.13) | copy-start | bytes 28
  45.7 243.7 %all-to-all-start = ((bf16[1,16,4,4,128,256]{5,4,3,2,0,1:T(8,128)(2,1)}), bf16[1,16,4,4,128,256]{5,4,3,2,0,1:T(8,128)(2,1)}, u32[]{:S(2)}, u32[]{:S(2)}) async-start(bf16[1,16,4,4,128,256]{5,4,3,2,0,1:T(8,128)(2,1)} %fusion), calls=%async_computation | async-start | bytes 33554432 | tf_op jit(solution)/shard_map/all_to_all | solution.py:115
  295.8 24.0 %copy-start.5 = (bf16[4,4,4,128]{3,2,1,0:T(4,128)(2,1)S(1)}, bf16[4,4,4,128]{3,2,1,0:T(4,128)(2,1)}, u32[]{:S(2)}) copy-start(bf16[4,4,4,128]{3,2,1,0:T(4,128)(2,1)} %param.14) | copy-start | bytes 49156
  319.8 18.9 %copy-start.4 = (bf16[3,3,128,128]{3,2,1,0:T(8,128)(2,1)S(1)}, bf16[3,3,128,128]{3,2,1,0:T(8,128)(2,1)}, u32[]{:S(2)}) copy-start(bf16[3,3,128,128]{3,2,1,0:T(8,128)(2,1)} %param.15) | copy-start | bytes 884740
  368.5 6.9 %copy-start.1 = (f32[256,7]{0,1:T(8,128)S(1)}, f32[256,7]{0,1:T(8,128)}, u32[]{:S(2)}) copy-start(f32[256,7]{0,1:T(8,128)} %param.19) | copy-start | bytes 21508
  376.9 11.4 %all-to-all-start.1 = ((f32[1,16,4,7]{3,2,0,1:T(4,128)}), f32[1,16,4,7]{3,2,0,1:T(4,128)S(1)}, u32[]{:S(2)}, u32[]{:S(2)}) async-start(f32[1,16,4,7]{3,2,0,1:T(4,128)} %fusion.5), calls=%async_computation.1 | async-start | bytes 65536 | tf_op jit(solution)/shard_map/all_to_all | solution.py:124
  389.2 11.7 %collective-permute-start.1 = (f32[2,7]{1,0:T(2,128)S(1)}, f32[2,7]{1,0:T(2,128)S(1)}, u32[]{:S(2)}, u32[]{:S(2)}) collective-permute-start(f32[2,7]{1,0:T(2,128)S(1)} %gather_fusion.2), channel_id=1, source_target_pairs={{16,0},{32,16},{48,32},{64,48},{80,64},{96,80},{112,96},{17,1},{33... | collective-permute-start | bytes 176 | tf_op jit(solution)/shard_map/ppermute | solution.py:25
  397.8 3.7 collective-permute-start
  402.8 6.1 %collective-permute-start.3 = (f32[2,7]{1,0:T(2,128)S(1)}, f32[2,7]{1,0:T(2,128)S(1)}, u32[]{:S(2)}, u32[]{:S(2)}) collective-permute-start(f32[2,7]{1,0:T(2,128)S(1)} %gather_fusion.4), channel_id=1, source_target_pairs={{16,0},{32,16},{48,32},{64,48},{80,64},{96,80},{112,96},{17,1},{33... | collective-permute-start | bytes 176 | tf_op jit(solution)/shard_map/ppermute | solution.py:25
  404.7 4.9 %collective-permute-start.2 = (f32[2,7]{1,0:T(2,128)S(1)}, f32[2,7]{1,0:T(2,128)S(1)}, u32[]{:S(2)}, u32[]{:S(2)}) collective-permute-start(f32[2,7]{1,0:T(2,128)S(1)} %gather_fusion.4), channel_id=1, source_target_pairs={{0,16},{16,32},{32,48},{48,64},{64,80},{80,96},{96,112},{1,17},{17... | collective-permute-start | bytes 176 | tf_op jit(solution)/shard_map/ppermute | solution.py:22
where the time goes:
time: 412 us; the launch traced here: 411 us
  waiting for transfers between devices  245 us (59%)
  matrix products  51.4 us (12%)
  local copies, waits for them, and re-layouts  45.6 us (11%)
  starting transfers between devices  28 us (7%)
  other arithmetic  22.6 us (5%)
  blocking collectives  14.8 us (4%)
    all_to_all x1, waiting for transfers between devices, per_device(): lax.all_to_all(outgoing, 'cnn', split_axis=1, concat_axis=1, tiled=True)  238 us
    conv_general_dilated x4, matrix products, convolve(): lax.conv_general_dilated(inputs, kernel, strides, padding_mode, dimension...  51.2 us
    reshape x1, local copies, waits for them, and re-layouts, per_device(): gathered.reshape((BAL * VIEWS,) + view_shape)  24 us
    concatenate x1, other arithmetic, send_order(): return jnp.roll(shaped, first_rank, axis=1)  16 us
    reshape x1, blocking collectives, per_device(): lax.all_gather(live_counts, 'cnn', axis=1, tiled=True).reshape(peer_count)  14.8 us
    ppermute x2, starting transfers between devices, with_halo(): lax.ppermute(lax.slice_in_dim(block, 0, width, axis=dim), axis, backward)  10.6 us
    reshape x1, local copies, waits for them, and re-layouts, send_order(): jnp.pad(units, padding).reshape((rounds, peer_count) + units.shape[1:])  9.34 us
  transfers between devices with their start and end apart: 6, of which 4 were waited for; matrix products, arithmetic and copies ran while one was open for 0% of the time, Pallas kernels for 0%

commit v1 on v0

v1 whole, which is shorter than its diff:
```python
import functools

import jax
import jax.numpy as jnp
from jax import lax
from jax.experimental import pallas as pl
from jax.experimental.pallas import tpu as pltpu
from jax.sharding import PartitionSpec as P

BF = jnp.bfloat16
F32 = jnp.float32
I32 = jnp.int32
MESH = pl.DeviceIdType.MESH
VMEM = pl.BlockSpec(memory_space=pltpu.VMEM)
SMEM = pl.BlockSpec(memory_space=pltpu.SMEM)
ANY = pl.BlockSpec(memory_space=pl.ANY)

VIEWS = 4
SLOTS = 8
RIM = 2
DEGREE = 4
ITERS = 2
CLASSES = 7
PAIR = 2
DIRS = 7
BACK = (0, 2, 1, 4, 3, 6, 5)
GOAL = 3
MOST = (2, 1)
ROUNDS = 4
OWN = DIRS - 1
OWN_LATE = OWN + SLOTS - 1
PLACES = DIRS + 2 * (SLOTS - 1)
FULL = (0, 256)


def dot(a, b):
    return jnp.dot(a, b, preferred_element_type=F32)


def rows_down(x):
    group = lax.broadcasted_iota(I32, x.shape, 0) % 16
    return jnp.where(group == 0, 0.0, pltpu.roll(x, 1, 0))


def rows_up(x):
    group = lax.broadcasted_iota(I32, x.shape, 0) % 16
    return jnp.where(group == 15, 0.0, pltpu.roll(x, x.shape[0] - 1, 0))


def prepare(patch_w, w1, w2, sel, wp, w1p, w2p, *maps):
    row = lax.broadcasted_iota(I32, (256, 256), 0)
    col = lax.broadcasted_iota(I32, (256, 256), 1)
    want = 16 * (row % 16) + 4 * ((row // 16) % 4) + row // 64
    sel[...] = jnp.where(col == want, 1.0, 0.0).astype(BF)
    row = lax.broadcasted_iota(I32, (512, 64), 0)
    col = lax.broadcasted_iota(I32, (512, 64), 1)
    dx, ch, dy = row // 128, (row // 32) % 4, row % 4
    spread = dot(jnp.where(col == dy * 16 + dx * 4 + ch, 1.0, 0.0).astype(BF), patch_w[...])
    r_of = (lax.broadcasted_iota(I32, (512, 128), 0) % 32) // 4
    for r in range(8):
        wp[:, r * 128 : (r + 1) * 128] = jnp.where(r_of == r, spread, 0.0).astype(BF)
    zero = jnp.zeros((128, 128), BF)
    for w, out in ((w1, w1p), (w2, w2p)):
        for dy in range(3):
            base = dy * 512
            for i, (even, odd) in enumerate(((1, 0), (2, 1), (0, None), (None, 2))):
                rows = pl.ds(base + i * 128, 128)
                out[rows, 0:128] = zero if even is None else w[dy, even]
                out[rows, 128:256] = zero if odd is None else w[dy, odd]
    for ref in maps:
        last = ref.shape[1] - 1
        for n in range(ref.shape[0]):
            ref[n, 0] = jnp.zeros(ref.shape[2:], BF)
            ref[n, last] = jnp.zeros(ref.shape[2:], BF)


def taps(parts, first, rows):
    pieces = []
    for dy in range(3):
        for ref, lanes in parts:
            piece = ref[pl.ds(first + dy, rows), :, lanes[0] : lanes[1]]
            pieces.append(piece.reshape(rows * piece.shape[1], piece.shape[2]))
    return jnp.concatenate(pieces, axis=1)


def tile_stage(load, sel, wp, xc, xs):
    pixels = jnp.concatenate([load(ch, 32 * b, 32) for b in range(4) for ch in range(4)], axis=0)
    moved = lax.dot_general(
        sel[...], pixels, (((1,), (1,)), ((), ())), preferred_element_type=F32
    ).astype(BF)
    tiles = jnp.concatenate(
        [
            jnp.concatenate(
                [moved[dx * 64 : (dx + 1) * 64, b * 128 : (b + 1) * 128] for dx in range(4)], axis=1
            )
            for b in range(4)
        ],
        axis=0,
    )
    for n in range(4):
        out = jnp.maximum(dot(tiles, wp[:, n * 256 : (n + 1) * 256]), 0.0)
        for half in range(2):
            lanes = out[:, half * 128 : (half + 1) * 128]
            for b in range(4):
                r = 1 + b * 8 + n * 2 + half
                q = [lanes[b * 64 + i * 16 : b * 64 + (i + 1) * 16] for i in range(4)]
                qb = [v.astype(BF) for v in q]
                xc[r, 0:16, 0:128] = qb[0]
                xc[r, 0:16, 128:256] = qb[1]
                xc[r, 16:32, 0:128] = qb[2]
                xc[r, 16:32, 128:256] = qb[3]
                xs[r, 0:16, 0:128] = rows_down(q[3]).astype(BF)
                xs[r, 0:16, 128:256] = qb[2]
                xs[r, 16:32, 0:128] = qb[1]
                xs[r, 16:32, 128:256] = rows_up(q[0]).astype(BF)


def first_stage(chunk, w1p, xc, xs, yc, ys):
    out = jnp.maximum(dot(taps(((xc, FULL), (xs, FULL)), chunk * 8, 8), w1p[...]), 0.0)
    pooled = (out[:, 0:128] + out[:, 128:256]).reshape(4, 2, 32, 128)
    pooled = (pooled[:, 0] + pooled[:, 1]) * 0.25
    even, odd = pooled[:, 0:16], pooled[:, 16:32]
    rows = pl.ds(1 + chunk * 4, 4)
    yc[rows, :, 0:128] = even.astype(BF)
    yc[rows, :, 128:256] = odd.astype(BF)
    ys[rows, :, 0:128] = rows_down(odd.reshape(64, 128)).astype(BF).reshape(4, 16, 128)
    ys[rows, :, 128:256] = rows_up(even.reshape(64, 128)).astype(BF).reshape(4, 16, 128)


def second_stage(w2p, yc, ys, tc, ts):
    out = jnp.maximum(dot(taps(((yc, FULL), (ys, FULL)), 0, 16), w2p[...]), 0.0)
    tc[1:17] = out.astype(BF).reshape(16, 16, 256)
    ts[1:17, :, 0:128] = rows_down(out[:, 128:256]).astype(BF).reshape(16, 16, 128)
    ts[1:17, :, 128:256] = rows_up(out[:, 0:128]).astype(BF).reshape(16, 16, 128)


def third_stage(w3, tc, ts, fe, fo, fm, fp):
    even = jnp.maximum(dot(taps(((ts, (0, 128)), (tc, FULL)), 0, 16), w3[...]), 0.0)
    odd = jnp.maximum(dot(taps(((tc, FULL), (ts, (128, 256))), 0, 16), w3[...]), 0.0)
    fe[1:17] = even.astype(BF).reshape(16, 16, 256)
    fo[1:17] = odd.astype(BF).reshape(16, 16, 256)
    fm[1:17] = rows_down(odd).astype(BF).reshape(16, 16, 256)
    fp[1:17] = rows_up(even).astype(BF).reshape(16, 16, 256)


def fourth_stage(w4, fe, fo, fm, fp):
    even = jnp.maximum(dot(taps(((fm, FULL), (fe, FULL), (fo, FULL)), 0, 16), w4[...]), 0.0)
    odd = jnp.maximum(dot(taps(((fe, FULL), (fo, FULL), (fp, FULL)), 0, 16), w4[...]), 0.0)
    return jnp.sum(even + odd, axis=0, keepdims=True) * (1.0 / 512)


def pair_feature(loads, w3, w4, sel, wp, w1p, w2p, *maps):
    own = [[m.at[v] for m in maps] for v in range(PAIR)]
    for v in range(PAIR):
        tile_stage(loads[v], sel, wp, *own[v][0:2])
    for chunk in range(4):
        for v in range(PAIR):
            first_stage(chunk, w1p, *own[v][0:4])
    for v in range(PAIR):
        second_stage(w2p, *own[v][2:6])
    for v in range(PAIR):
        third_stage(w3, *own[v][4:10])
    features = [fourth_stage(w4, *own[v][6:10]) for v in range(PAIR)]
    return features[0] + features[1]


def net_scratch():
    shapes = [(256, 256), (512, 1024), (1536, 256), (1536, 256)]
    shapes += [(PAIR, 34, 32, 256)] * 2 + [(PAIR, 18, 16, 256)] * 8
    return [pltpu.VMEM(shape, BF) for shape in shapes]


def neighbours():
    s, c = lax.axis_index("span"), lax.axis_index("cnn")
    z, y = c // 4, c % 4
    return (
        (s + 1 - 2 * (s % 2), c),
        ((s + 2) % 8, c),
        ((s + 6) % 8, c),
        (s, (c + 4) % 16),
        (s, (c + 12) % 16),
        (s, z * 4 + (y + 1) % 4),
        (s, z * 4 + (y + 3) % 4),
    )


def seen(d, v):
    def ahead(n):
        return pltpu.roll(v, (128 - n) % 128, 1)

    g = lax.broadcasted_iota(I32, v.shape, 1)
    if d == 0:
        return jnp.where(g % 32 < 16, ahead(16), ahead(112))
    if d == 1:
        return ahead(32)
    if d == 2:
        return ahead(96)
    if d == 3:
        return jnp.where(g % 16 < 12, ahead(4), ahead(116))
    if d == 4:
        return jnp.where(g % 16 >= 4, ahead(124), ahead(12))
    if d == 5:
        return jnp.where(g % 4 < 3, ahead(1), ahead(125))
    return jnp.where(g % 4 >= 1, ahead(127), ahead(3))


def make_plan(counts):
    extra = counts - 1
    divisor = jnp.maximum(extra, 1)
    bit = []
    for d in range(DIRS):
        rest = jnp.full_like(counts, d)
        for _ in range(d):
            rest = jnp.where(rest >= divisor, rest - divisor, rest)
        bit.append(jnp.left_shift(jnp.ones_like(counts), 1 + rest))
    zero = jnp.zeros_like(counts)
    load = 2 * extra
    passed, taken, number = [zero, zero], [zero, zero], [zero, zero]
    for turn in range(ROUNDS):
        if turn:
            over = (load > GOAL).astype(I32)
            near = zero
            for d in range(DIRS):
                near = near | seen(d, over)
        for half in (0, 1) if turn % 2 == 0 else (1, 0):
            for d in range(DIRS) if turn % 2 == 0 else reversed(range(DIRS)):
                room = jnp.where((number[half] < MOST[half]) & (load < GOAL), load, 99)
                there = seen(d, room)
                wish = load > GOAL
                if turn:
                    wish = wish | ((load == GOAL) & (near > 0)) | (load - there >= 2)
                push = wish & (there < 99) & ((passed[half] & bit[d]) == 0) & (extra > 0)
                gone = push.astype(I32)
                come = seen(BACK[d], gone)
                passed[half] = passed[half] | (gone * bit[d])
                taken[half] = taken[half] | (come << BACK[d])
                number[half] = number[half] + come
                load = load - gone + come
    return passed, taken


def lowest(mask, places):
    place = jnp.int32(-1)
    for i in reversed(range(places)):
        place = jnp.where((mask >> i) & 1 == 1, jnp.int32(i), place)
    return place


def label_kernel(
    views, count, patch_w, w1, w2, w3, w4, head,
    total_out, left_out,
    own0, own_a, own_b, own_c, own_d, early, late, send, mine, x_in, c_mine, c_in, back_out, back_in,
    sel, wp, w1p, w2p, m0, m1, m2, m3, m4, m5, m6, m7, m8, m9,
    own_sem, local_sem, view_send, view_recv, x_send, x_recv, c_send, c_recv, b_send, b_recv,
):
    net = (sel, wp, w1p, w2p, m0, m1, m2, m3, m4, m5, m6, m7, m8, m9)
    s, c = lax.axis_index("span"), lax.axis_index("cnn")
    near = neighbours()
    along_x = [((s + o) % 8, c) for o in range(1, 8)]
    along_c = [(s, (c + o) % 16) for o in range(1, 16)]

    own_copy = pltpu.make_async_copy(views.at[0], own0, own_sem)
    own_copy.start()
    own = ((own_a, own_b), (own_c, own_d))
    copies = []
    for half in range(2):
        for j in range(PAIR):
            copies.append(
                pltpu.make_async_copy(
                    views.at[pl.ds(1, SLOTS - 1), half * PAIR + j], own[half][j], local_sem.at[half, j]
                )
            )
            copies[-1].start()

    barrier = pltpu.get_barrier_semaphore()
    for other in along_x + along_c:
        pl.semaphore_signal(barrier, inc=1, device_id=other, device_id_type=MESH)
    pl.semaphore_wait(barrier, len(along_x) + len(along_c))

    own_count = count[0, 0]
    me = s * 16 + c
    lane = lax.broadcasted_iota(I32, (8, 128), 1)
    mine[...] = jnp.where(lane == me, own_count, 0)
    x_copies = []
    for o in range(7):
        x_copies.append(
            pltpu.make_async_remote_copy(
                src_ref=mine, dst_ref=x_in.at[o], send_sem=x_send.at[o], recv_sem=x_recv.at[o],
                device_id=along_x[o], device_id_type=MESH,
            )
        )
        x_copies[-1].start()

    divisor = jnp.maximum(own_count - 1, 1)
    slot = [jnp.int32(1) + lax.rem(jnp.int32(d), divisor) for d in range(DIRS)]
    view_copies = [[], []]
    for half in range(2):
        for j in range(PAIR):
            copies[half * PAIR + j].wait()
            for d in range(DIRS):
                for ch in range(4):
                    send[half, j, d, ch] = own[half][j][jnp.clip(slot[d] - 1, 0, SLOTS - 2), ch]
                target = (early, late)[half].at[j, BACK[d]]
                copy = pltpu.make_async_remote_copy(
                    src_ref=send.at[half, j, d], dst_ref=target,
                    send_sem=view_send.at[half, j, d], recv_sem=view_recv.at[half, j, BACK[d]],
                    device_id=near[d], device_id_type=MESH,
                )
                copy.start()
                view_copies[half].append(copy)

    prepare(patch_w, w1, w2, *net)
    for copy in x_copies:
        copy.wait()
    total = mine[...]
    for o in range(7):
        total = total + x_in[o]
    c_mine[...] = total
    c_copies = []
    for o in range(15):
        c_copies.append(
            pltpu.make_async_remote_copy(
                src_ref=c_mine, dst_ref=c_in.at[o], send_sem=c_send.at[o], recv_sem=c_recv.at[o],
                device_id=along_c[o], device_id_type=MESH,
            )
        )
        c_copies[-1].start()

    own_copy.wait()

    def own_pair(half):
        loads = [
            lambda ch, first, rows, v=half * PAIR + j: own0[v, ch, pl.ds(first, rows), :]
            for j in range(PAIR)
        ]
        return pair_feature(loads, w3, w4, *net)

    units = [own_pair(0)]
    for copy in c_copies:
        copy.wait()
    counts = c_mine[...]
    for o in range(15):
        counts = counts + c_in[o]
    passed, taken = make_plan(counts)

    def here(v):
        return jnp.sum(jnp.where((lane == me)[0:1], v[0:1], 0))

    live = (jnp.left_shift(jnp.int32(1), own_count) - 1) & 254
    kept = [live & ~here(passed[half]) for half in range(2)]
    got = [here(taken[half]) for half in range(2)]
    units.append(own_pair(1))

    first_mask = got[0] | ((kept[0] >> 1) << DIRS) | ((kept[1] >> 1) << (OWN_LATE + 1))
    picks = []
    for _ in range(GOAL):
        pick = lowest(first_mask, PLACES)
        picks.append(pick)
        first_mask = first_mask & ~jnp.where(
            pick >= 0, jnp.left_shift(jnp.int32(1), jnp.maximum(pick, 0)), 0
        )
    late_dir = lowest(got[1], DIRS)
    has_late = late_dir >= 0
    third = picks[2]
    first_mask = first_mask | jnp.where(
        has_late & (third >= 0), jnp.left_shift(jnp.int32(1), jnp.maximum(third, 0)), 0
    )
    picks[2] = jnp.where(has_late, PLACES + late_dir, third)

    for copy in view_copies[0]:
        copy.wait()

    def at_place(place, j, ch, first, rows):
        pixels = [
            ref[jnp.clip(place - base, 0, DIRS - 1), ch, pl.ds(first, rows), :]
            for ref, base in ((early.at[j], 0), (own[0][j], OWN + 1), (own[1][j], OWN_LATE + 1))
        ]
        return jnp.where(
            place <= OWN, pixels[0], jnp.where(place <= OWN_LATE, pixels[1], pixels[2])
        )

    for n in range(GOAL - 1):
        loads = [
            lambda ch, first, rows, j=j, n=n: at_place(picks[n], j, ch, first, rows)
            for j in range(PAIR)
        ]
        units.append(pair_feature(loads, w3, w4, *net))
    for copy in view_copies[1]:
        copy.wait()
    place_late = jnp.clip(late_dir, 0, DIRS - 1)
    loads = [
        lambda ch, first, rows, j=j: jnp.where(
            has_late,
            late[j, place_late, ch, pl.ds(first, rows), :],
            at_place(third, j, ch, first, rows),
        )
        for j in range(PAIR)
    ]
    units.append(pair_feature(loads, w3, w4, *net))

    units = jnp.concatenate(units + [jnp.zeros((8 - len(units), 256), F32)], axis=0)
    logits = (
        jnp.dot(units, head[...], preferred_element_type=F32, precision=lax.Precision.HIGHEST)
        * (1.0 / VIEWS)
    )
    logits = jnp.concatenate([logits, jnp.zeros((8, 128 - CLASSES), F32)], axis=1)
    row = lax.broadcasted_iota(I32, (8, 128), 0)
    result = jnp.where(row == 0, logits[0:1] + logits[1:2], 0.0)
    for n, pick in enumerate(picks):
        unit = logits[2 + n : 3 + n]
        for own in (OWN, OWN_LATE):
            is_own = (pick >= own + 1) & (pick < own + SLOTS)
            result = result + jnp.where(is_own & (row == pick - own), unit, 0.0)
    b_copies = []
    for d in range(DIRS):
        answer = jnp.zeros((8, 128), F32)
        for n, pick in enumerate(picks):
            ours = (pick == d) | (pick == PLACES + d)
            answer = answer + jnp.where(ours, logits[2 + n : 3 + n], 0.0)
        back_out[d] = answer
        b_copies.append(
            pltpu.make_async_remote_copy(
                src_ref=back_out.at[d], dst_ref=back_in.at[BACK[d]],
                send_sem=b_send.at[d], recv_sem=b_recv.at[BACK[d]],
                device_id=near[d], device_id_type=MESH,
            )
        )
        b_copies[-1].start()
    rest0 = (first_mask >> DIRS) & 127
    rest1 = (first_mask >> (OWN_LATE + 1)) & 127
    left_out[...] = jnp.where(lane == 0, rest0 | (rest1 << 7), 0)
    for copy in b_copies:
        copy.wait()
    for d in range(DIRS):
        result = result + jnp.where(row == slot[d], back_in[d], 0.0)
    total_out[...] = result


def label(views, count, patch_w, w1, w2, w3, w4, head):
    dma = pltpu.SemaphoreType.DMA
    pixels = (4, 128, 256)
    tile = (8, 128)
    return pl.pallas_call(
        label_kernel,
        out_shape=(jax.ShapeDtypeStruct(tile, F32), jax.ShapeDtypeStruct(tile, I32)),
        in_specs=[ANY, SMEM] + [VMEM] * 6,
        out_specs=(VMEM, VMEM),
        scratch_shapes=[
            pltpu.VMEM((VIEWS, *pixels), BF),
            *[pltpu.VMEM((SLOTS - 1, *pixels), BF)] * (2 * PAIR),
            pltpu.VMEM((PAIR, DIRS, *pixels), BF),
            pltpu.VMEM((PAIR, DIRS, *pixels), BF),
            pltpu.VMEM((2, PAIR, DIRS, *pixels), BF),
            pltpu.VMEM(tile, I32),
            pltpu.VMEM((7, *tile), I32),
            pltpu.VMEM(tile, I32),
            pltpu.VMEM((15, *tile), I32),
            pltpu.VMEM((DIRS, *tile), F32),
            pltpu.VMEM((DIRS, *tile), F32),
            *net_scratch(),
            dma(()), dma((2, PAIR)),
            dma((2, PAIR, DIRS)), dma((2, PAIR, DIRS)),
            dma((7,)), dma((7,)), dma((15,)), dma((15,)), dma((DIRS,)), dma((DIRS,)),
        ],
        compiler_params=pltpu.CompilerParams(
            collective_id=0, has_side_effects=True, vmem_limit_bytes=58 << 20
        ),
    )(views, count, patch_w, w1, w2, w3, w4, head)


def rest_kernel(
    left, views, patch_w, w1, w2, w3, w4, head, total,
    total_out, own, pw_v, w1_v, w2_v, w3_v, w4_v, *net_and_sems,
):
    net, sems = net_and_sems[:-1], net_and_sems[-1]
    mask = left[0, 0]
    total_out[...] = total[...]

    @pl.when(mask != 0)
    def _():
        moves = [
            pltpu.make_async_copy(a, b, sems.at[i])
            for i, (a, b) in enumerate(
                ((patch_w, pw_v), (w1, w1_v), (w2, w2_v), (w3, w3_v), (w4, w4_v))
            )
        ]
        for move in moves:
            move.start()
        for move in moves:
            move.wait()
        prepare(pw_v, w1_v, w2_v, *net)

        @pl.loop(0, 2 * (SLOTS - 1))
        def _(i):
            @pl.when((mask >> i) & 1 == 1)
            def _():
                slot, half = 1 + i % (SLOTS - 1), i // (SLOTS - 1)
                move = pltpu.make_async_copy(
                    views.at[slot, pl.ds(half * PAIR, PAIR)], own, sems.at[5]
                )
                move.start()
                move.wait()
                loads = [
                    lambda ch, first, rows, v=j: own[v, ch, pl.ds(first, rows), :]
                    for j in range(PAIR)
                ]
                unit = jnp.broadcast_to(pair_feature(loads, w3_v, w4_v, *net), (8, 256))
                logits = (
                    jnp.dot(unit, head[...], preferred_element_type=F32, precision=lax.Precision.HIGHEST)
                    * (1.0 / VIEWS)
                )
                logits = jnp.concatenate([logits, jnp.zeros((8, 128 - CLASSES), F32)], axis=1)
                row = lax.broadcasted_iota(I32, (8, 128), 0)
                total_out[...] += jnp.where(row == slot, logits, 0.0)


def rest(left, views, patch_w, w1, w2, w3, w4, head, total):
    pixels = (4, 128, 256)
    return pl.pallas_call(
        rest_kernel,
        out_shape=jax.ShapeDtypeStruct((8, 128), F32),
        in_specs=[SMEM] + [ANY] * 6 + [VMEM] * 2,
        out_specs=VMEM,
        scratch_shapes=[
            pltpu.VMEM((PAIR, *pixels), BF),
            pltpu.VMEM(patch_w.shape, BF),
            pltpu.VMEM(w1.shape, BF),
            pltpu.VMEM(w2.shape, BF),
            pltpu.VMEM(w3.shape, BF),
            pltpu.VMEM(w4.shape, BF),
            *net_scratch(),
            pltpu.SemaphoreType.DMA((6,)),
        ],
        compiler_params=pltpu.CompilerParams(vmem_limit_bytes=40 << 20),
    )(left, views, patch_w, w1, w2, w3, w4, head, total)


def remainder(x, n, bound):
    for _ in range(bound - 1):
        x = jnp.where(x >= n, x - n, x)
    return x


def smooth_kernel(total, count, edges, bounds, labels, rim_out, rim_in, send_sem, recv_sem):
    s, c = lax.axis_index("span"), lax.axis_index("cnn")
    above, below = ((s + 1) % 8, c), ((s + 7) % 8, c)
    barrier = pltpu.get_barrier_semaphore()
    for other in (above, below):
        pl.semaphore_signal(barrier, inc=1, device_id=other, device_id_type=MESH)
    own_count = count[0, 0]
    row = lax.broadcasted_iota(I32, (8, 128), 0)
    alive = row < own_count
    smooth = jnp.where(alive, total[...], 0.0)
    border = 2 * RIM
    edge = edges[...]
    lookup = jnp.where(
        edge < border, edge, border + remainder(edge - border, own_count, SLOTS)
    )
    share = []
    for r in range(border + SLOTS):
        hits = (lookup == r).astype(F32)
        weight = hits[:, 0:1]
        for k in range(1, DEGREE):
            weight = weight + hits[:, k : k + 1]
        share.append(weight * (1.0 / DEGREE))
    exported_ids = [remainder(bounds[r], own_count, SLOTS) for r in range(RIM)]
    pl.semaphore_wait(barrier, 2)
    for step in range(ITERS):
        exported = jnp.zeros((8, 128), F32)
        for r in range(RIM):
            line = jnp.sum(jnp.where(row == exported_ids[r], smooth, 0.0), axis=0, keepdims=True)
            exported = jnp.where(row == r, line, exported)
        rim_out[step] = exported
        copies = []
        for side, other in enumerate((above, below)):
            copies.append(
                pltpu.make_async_remote_copy(
                    src_ref=rim_out.at[step], dst_ref=rim_in.at[step, side],
                    send_sem=send_sem.at[step, side], recv_sem=recv_sem.at[step, side],
                    device_id=other, device_id_type=MESH,
                )
            )
            copies[-1].start()
        mean = jnp.zeros((8, 128), F32)
        for r in range(SLOTS):
            mean = mean + share[border + r] * smooth[r : r + 1]
        for copy in copies:
            copy.wait()
        from_below = jnp.where(s > 0, rim_in[step, 0], 0.0)
        from_above = jnp.where(s < 7, rim_in[step, 1], 0.0)
        for r in range(RIM):
            mean = mean + share[r] * from_below[r : r + 1]
            mean = mean + share[RIM + r] * from_above[r : r + 1]
        smooth = jnp.where(alive, 0.5 * smooth + 0.5 * mean, 0.0)
    labels[...] = smooth[:, 0:CLASSES]


def smoothing(total, count, edges, bounds):
    dma = pltpu.SemaphoreType.DMA
    return pl.pallas_call(
        smooth_kernel,
        out_shape=jax.ShapeDtypeStruct((SLOTS, CLASSES), F32),
        in_specs=[VMEM, SMEM, VMEM, SMEM],
        out_specs=VMEM,
        scratch_shapes=[
            pltpu.VMEM((ITERS, 8, 128), F32),
            pltpu.VMEM((ITERS, 2, 8, 128), F32),
            dma((ITERS, 2)),
            dma((ITERS, 2)),
        ],
        compiler_params=pltpu.CompilerParams(collective_id=1, has_side_effects=True),
    )(total, count, edges, bounds)


def per_device(
    views, live_counts, skeleton_edges, boundary_rows,
    patch_weight, conv_first, conv_second, conv_third, conv_fourth, head_weight,
):
    weights = (
        patch_weight.reshape(64, 128),
        conv_first,
        conv_second,
        conv_third.reshape(1152, 256),
        conv_fourth.reshape(2304, 256),
        head_weight,
    )
    total, left = label(views, live_counts, *weights)
    total = rest(left, views, *weights, total)
    return smoothing(total, live_counts, skeleton_edges, boundary_rows)


def solution(mesh):
    placed = (
        P(("span", "cnn"), None, None, None, None),
        P("span", "cnn"),
        P(("span", "cnn"), None),
        P(("span", "cnn")),
        P(),
        P(),
        P(),
        P(),
        P(),
        P(),
    )
    return jax.shard_map(
        per_device, mesh=mesh, in_specs=placed, out_specs=P(("span", "cnn"), None), check_vma=False
    )
```

time: 412 us -> 83.6 us (0.20)
  waiting for transfers between devices: 245 us -> 0 us
  Pallas kernels: 0 us -> 73.5 us
  matrix products: 51.4 us -> 0 us
  local copies, waits for them, and re-layouts: 45.6 us -> 8.91 us
  starting transfers between devices: 28 us -> 0 us
  other arithmetic: 22.6 us -> 0 us
  blocking collectives: 14.8 us -> 0 us
    all_to_all x2 -> x0, waiting for transfers between devices: 244 us -> none  [the longest x1 238 us: per_device(): lax.all_to_all(outgoing, 'cnn', split_axis=1, concat_axis=1, tiled=True)]
    pallas_call x0 -> x3, Pallas kernels: none -> 73.5 us  [the longest x1 63.6 us: label(): pl.pallas_call(label_kernel, out_shape=(jax.ShapeDtypeStruct(tile, F32),...]
    conv_general_dilated x4 -> x0, matrix products: 51.2 us -> none  [convolve(): lax.conv_general_dilated(inputs, kernel, strides, padding_mode, dimension...]
    reshape x3 -> x0, local copies, waits for them, and re-layouts: 33.4 us -> none  [the longest x1 24 us: per_device(): gathered.reshape((BAL * VIEWS,) + view_shape)]
    ppermute x4 -> x0, starting transfers between devices: 17.8 us -> none  [the longest x2 10.6 us: with_halo(): lax.ppermute(lax.slice_in_dim(block, 0, width, axis=dim), axis, backward)]
    concatenate x3 -> x0, other arithmetic: 16 us -> none  [the longest x1 16 us: send_order(): return jnp.roll(shaped, first_rank, axis=1)]
    reshape x1 -> x0, blocking collectives: 14.8 us -> none  [per_device(): lax.all_gather(live_counts, 'cnn', axis=1, tiled=True).reshape(peer_count)]
    all_to_all x2 -> x0, starting transfers between devices: 10.2 us -> none  [the longest x1 5.29 us: per_device(): lax.all_to_all(outgoing, 'cnn', split_axis=1, concat_axis=1, tiled=True)]
  transfers between devices with their start and end apart: 6 -> 0, of which waited for: 4 -> 0; matrix products, arithmetic and copies ran while one was open for 0% -> 0% of each run, Pallas kernels for 0% -> 0%
where the time goes in v1:
time: 83.6 us; the launch traced here: 83.3 us
  Pallas kernels  73.5 us (88%)
  local copies, waits for them, and re-layouts  8.91 us (11%)
    pallas_call x1, Pallas kernels, label(): pl.pallas_call(label_kernel, out_shape=(jax.ShapeDtypeStruct(tile, F32),...  63.6 us
    pallas_call x1, Pallas kernels, smoothing(): pl.pallas_call(smooth_kernel, out_shape=jax.ShapeDtypeStruct((SLOTS, CLAS...  9.05 us
    unnamed x25, local copies, waits for them, and re-layouts  8.91 us

profile of v1, /device:TPU:1, one launch (start us, length us, event | category | flops | bytes accessed | tf_op | source)
XLA Modules:
  0.0 83.3 jit_solution(15326132858563689059)
XLA Ops:
  0.0 0.0 copy-start.6
  0.0 0.0 copy-start.2
  0.0 0.0 copy-start.4
  0.0 0.0 copy-start.5
  0.0 1.6 %copy.11.head = f32[256,7]{1,0:T(8,128)} copy(f32[256,7]{0,1:T(8,128)} %param.19) | data formatting | bytes 14336 | tf_op args[9]
  2.3 0.0 copy-start.10
  2.4 63.6 %shard_map.100 = (f32[8,128]{1,0:T(8,128)}, s32[8,128]{1,0:T(8,128)}) custom-call(bf16[8,4,4,128,256]{4,3,2,1,0:T(8,128)(2,1)} %views.3, s32[1,1]{1,0:T(1,128)S(6)} %copy.15.count, bf16[64,128]{1,0:T(8,128)(2,1)} %bitcast.7, bf16[3,3,128,128]{3,2,1,0:T(8,128)(2,1)} %w1.3, bf16[3,3,128,128]{3,2,1,0:T(8,128)(2,1)} %w2.3, bf16[1152,256]{1,0:T(8,128)(2,1)} %bitcast.5, ...), custom_call_target="tpu_custom_call" | custom-call | tf_op jit(solution)/shard_map/pallas_call | solution.py:443
  66.0 0.0 copy-done.6
  66.0 0.0 copy-done.2
  66.0 0.0 copy-done.1
  66.0 0.0 copy-done.4
  66.0 0.0 copy-done.5
  66.0 0.0 copy-done.3
  66.0 0.0 copy-start
  66.0 3.4 %copy-done = bf16[8,4,4,128,256]{4,3,2,1,0:T(8,128)(2,1)S(1)} copy-done((bf16[8,4,4,128,256]{4,3,2,1,0:T(8,128)(2,1)S(1)}, bf16[8,4,4,128,256]{4,3,2,1,0:T(8,128)(2,1)}, u32[]{:S(2)}) %copy-start) | copy-done | bytes 8388632
  69.4 0.7 copy-done.8
  70.1 0.7 copy-done.9
  70.8 0.9 %shard_map.101.total = f32[8,128]{1,0:T(8,128)S(1)} custom-call(s32[8,128]{1,0:T(8,128)S(1)} %copy-done.9, bf16[8,4,4,128,256]{4,3,2,1,0:T(8,128)(2,1)S(1)} %copy-done, bf16[64,128]{1,0:T(8,128)(2,1)S(1)} %bitcast.8, bf16[3,3,128,128]{3,2,1,0:T(8,128)(2,1)S(1)} %copy-done.4, bf16[3,3,128,128]{3,2,1,0:T(8,128)(2,1)S(1)} %copy-done.5, ...), custom_call_target="tpu_custom_call" | custom-call | tf_op jit(solution)/shard_map/pallas_call | solution.py:519
  71.7 0.0 copy-start.7
  71.7 0.6 copy-done.7
  72.3 0.0 copy-done.10
  72.3 0.7 copy.13.edges
  72.9 9.1 %shard_map.102 = f32[8,7]{1,0:T(8,128)} custom-call(f32[8,128]{1,0:T(8,128)} %copy-done.7, s32[1,1]{1,0:T(1,128)S(6)} %copy.15.count, s32[8,4]{1,0:T(8,128)} %copy.13.edges, s32[2]{0:T(128)} %bounds.1), custom_call_target="tpu_custom_call" | custom-call | tf_op jit(solution)/shard_map/pallas_call | solution.py:600
  82.0 1.3 %copy.16 = f32[8,7]{1,0:T(8,128)} copy(f32[8,7]{1,0:T(8,128)} %shard_map.102) | data formatting | bytes 448
  (4 shorter events, 0.0 us)
Async XLA Ops:
  0.0 66.0 %copy-start.6 = (bf16[4,4,4,128]{3,2,1,0:T(4,128)(2,1)S(1)}, bf16[4,4,4,128]{3,2,1,0:T(4,128)(2,1)}, u32[]{:S(2)}) copy-start(bf16[4,4,4,128]{3,2,1,0:T(4,128)(2,1)} %param.14) | copy-start | bytes 49156
  0.0 66.0 %copy-start.2 = (bf16[3,3,128,256]{3,2,1,0:T(8,128)(2,1)S(1)}, bf16[3,3,128,256]{3,2,1,0:T(8,128)(2,1)}, u32[]{:S(2)}) copy-start(bf16[3,3,128,256]{3,2,1,0:T(8,128)(2,1)} %param.17) | copy-start | bytes 1769476
  0.0 66.0 %copy-start.1 = (bf16[3,3,256,256]{3,2,1,0:T(8,128)(2,1)S(1)}, bf16[3,3,256,256]{3,2,1,0:T(8,128)(2,1)}, u32[]{:S(2)}) copy-start(bf16[3,3,256,256]{3,2,1,0:T(8,128)(2,1)} %param.18) | copy-start | bytes 3538948
  0.0 66.0 %copy-start.4 = (bf16[3,3,128,128]{3,2,1,0:T(8,128)(2,1)S(1)}, bf16[3,3,128,128]{3,2,1,0:T(8,128)(2,1)}, u32[]{:S(2)}) copy-start(bf16[3,3,128,128]{3,2,1,0:T(8,128)(2,1)} %w1.3) | copy-start | bytes 884740
  0.0 66.0 %copy-start.5 = (bf16[3,3,128,128]{3,2,1,0:T(8,128)(2,1)S(1)}, bf16[3,3,128,128]{3,2,1,0:T(8,128)(2,1)}, u32[]{:S(2)}) copy-start(bf16[3,3,128,128]{3,2,1,0:T(8,128)(2,1)} %w2.3) | copy-start | bytes 884740
  1.7 64.4 %copy-start.3 = (f32[256,7]{1,0:T(8,128)S(1)}, f32[256,7]{1,0:T(8,128)}, u32[]{:S(2)}) copy-start(f32[256,7]{1,0:T(8,128)} %copy.11.head) | copy-start | bytes 21508
  2.3 69.9 %copy-start.10 = (s32[8,4]{0,1:T(4,128)S(1)}, s32[8,4]{0,1:T(4,128)}, u32[]{:S(2)}) copy-start(s32[8,4]{0,1:T(4,128)} %param.12) | copy-start | bytes 388
  66.0 3.4 %copy-start = (bf16[8,4,4,128,256]{4,3,2,1,0:T(8,128)(2,1)S(1)}, bf16[8,4,4,128,256]{4,3,2,1,0:T(8,128)(2,1)}, u32[]{:S(2)}) copy-start(bf16[8,4,4,128,256]{4,3,2,1,0:T(8,128)(2,1)} %views.3) | copy-start | bytes 25165828
  69.4 0.7 copy-start.8
  70.1 0.7 copy-start.9
  71.7 0.6 copy-start.7

commit v2 on v1

v2 whole, which is shorter than its diff:
```python
import functools

import jax
import jax.numpy as jnp
from jax import lax
from jax.experimental import pallas as pl
from jax.experimental.pallas import tpu as pltpu
from jax.sharding import PartitionSpec as P

BF = jnp.bfloat16
F32 = jnp.float32
I32 = jnp.int32
MESH = pl.DeviceIdType.MESH
VMEM = pl.BlockSpec(memory_space=pltpu.VMEM)
SMEM = pl.BlockSpec(memory_space=pltpu.SMEM)
ANY = pl.BlockSpec(memory_space=pl.ANY)

VIEWS = 4
SLOTS = 8
RIM = 2
DEGREE = 4
ITERS = 2
CLASSES = 7
PAIR = 2
DIRS = 7
BACK = (0, 2, 1, 4, 3, 6, 5)
GOAL = 3
MOST = (3, 1)
ROUNDS = 4
ORDER = [(1, 0), (0, 0)] + [(half, d) for half in range(2) for d in range(1, DIRS)]
OWN = DIRS
OWN_LATE = OWN + SLOTS - 1
PLACES = OWN_LATE + SLOTS
FULL = (0, 256)


def dot(a, b):
    return jnp.dot(a, b, preferred_element_type=F32)


def rows_down(x):
    group = lax.broadcasted_iota(I32, x.shape, 0) % 16
    return jnp.where(group == 0, 0.0, pltpu.roll(x, 1, 0))


def rows_up(x):
    group = lax.broadcasted_iota(I32, x.shape, 0) % 16
    return jnp.where(group == 15, 0.0, pltpu.roll(x, x.shape[0] - 1, 0))


def prepare(patch_w, w1, w2, sel, wp, w1p, w2p, *maps):
    row = lax.broadcasted_iota(I32, (256, 256), 0)
    col = lax.broadcasted_iota(I32, (256, 256), 1)
    want = 16 * (row % 16) + 4 * ((row // 16) % 4) + row // 64
    sel[...] = jnp.where(col == want, 1.0, 0.0).astype(BF)
    row = lax.broadcasted_iota(I32, (512, 64), 0)
    col = lax.broadcasted_iota(I32, (512, 64), 1)
    dx, ch, dy = row // 128, (row // 32) % 4, row % 4
    spread = dot(jnp.where(col == dy * 16 + dx * 4 + ch, 1.0, 0.0).astype(BF), patch_w[...])
    r_of = (lax.broadcasted_iota(I32, (512, 128), 0) % 32) // 4
    for r in range(8):
        wp[:, r * 128 : (r + 1) * 128] = jnp.where(r_of == r, spread, 0.0).astype(BF)
    zero = jnp.zeros((128, 128), BF)
    for w, out in ((w1, w1p), (w2, w2p)):
        for dy in range(3):
            base = dy * 512
            for i, (even, odd) in enumerate(((1, 0), (2, 1), (0, None), (None, 2))):
                rows = pl.ds(base + i * 128, 128)
                out[rows, 0:128] = zero if even is None else w[dy, even]
                out[rows, 128:256] = zero if odd is None else w[dy, odd]
    for ref in maps:
        last = ref.shape[1] - 1
        for n in range(ref.shape[0]):
            ref[n, 0] = jnp.zeros(ref.shape[2:], BF)
            ref[n, last] = jnp.zeros(ref.shape[2:], BF)


def taps(parts, first, rows):
    pieces = []
    for dy in range(3):
        for ref, lanes in parts:
            piece = ref[pl.ds(first + dy, rows), :, lanes[0] : lanes[1]]
            pieces.append(piece.reshape(rows * piece.shape[1], piece.shape[2]))
    return jnp.concatenate(pieces, axis=1)


def tile_stage(load, sel, wp, xc, xs):
    pixels = jnp.concatenate([load(ch, 32 * b, 32) for b in range(4) for ch in range(4)], axis=0)
    moved = lax.dot_general(
        sel[...], pixels, (((1,), (1,)), ((), ())), preferred_element_type=F32
    ).astype(BF)
    tiles = jnp.concatenate(
        [
            jnp.concatenate(
                [moved[dx * 64 : (dx + 1) * 64, b * 128 : (b + 1) * 128] for dx in range(4)], axis=1
            )
            for b in range(4)
        ],
        axis=0,
    )
    for n in range(4):
        out = jnp.maximum(dot(tiles, wp[:, n * 256 : (n + 1) * 256]), 0.0)
        for half in range(2):
            lanes = out[:, half * 128 : (half + 1) * 128]
            for b in range(4):
                r = 1 + b * 8 + n * 2 + half
                q = [lanes[b * 64 + i * 16 : b * 64 + (i + 1) * 16] for i in range(4)]
                qb = [v.astype(BF) for v in q]
                xc[r, 0:16, 0:128] = qb[0]
                xc[r, 0:16, 128:256] = qb[1]
                xc[r, 16:32, 0:128] = qb[2]
                xc[r, 16:32, 128:256] = qb[3]
                xs[r, 0:16, 0:128] = rows_down(q[3]).astype(BF)
                xs[r, 0:16, 128:256] = qb[2]
                xs[r, 16:32, 0:128] = qb[1]
                xs[r, 16:32, 128:256] = rows_up(q[0]).astype(BF)


def first_stage(chunk, w1p, xc, xs, yc, ys):
    out = jnp.maximum(dot(taps(((xc, FULL), (xs, FULL)), chunk * 8, 8), w1p[...]), 0.0)
    pooled = (out[:, 0:128] + out[:, 128:256]).reshape(4, 2, 32, 128)
    pooled = (pooled[:, 0] + pooled[:, 1]) * 0.25
    even, odd = pooled[:, 0:16], pooled[:, 16:32]
    rows = pl.ds(1 + chunk * 4, 4)
    yc[rows, :, 0:128] = even.astype(BF)
    yc[rows, :, 128:256] = odd.astype(BF)
    ys[rows, :, 0:128] = rows_down(odd.reshape(64, 128)).astype(BF).reshape(4, 16, 128)
    ys[rows, :, 128:256] = rows_up(even.reshape(64, 128)).astype(BF).reshape(4, 16, 128)


def second_stage(w2p, yc, ys, tc, ts):
    out = jnp.maximum(dot(taps(((yc, FULL), (ys, FULL)), 0, 16), w2p[...]), 0.0)
    tc[1:17] = out.astype(BF).reshape(16, 16, 256)
    ts[1:17, :, 0:128] = rows_down(out[:, 128:256]).astype(BF).reshape(16, 16, 128)
    ts[1:17, :, 128:256] = rows_up(out[:, 0:128]).astype(BF).reshape(16, 16, 128)


def third_stage(w3, tc, ts, fe, fo, fm, fp):
    even = jnp.maximum(dot(taps(((ts, (0, 128)), (tc, FULL)), 0, 16), w3[...]), 0.0)
    odd = jnp.maximum(dot(taps(((tc, FULL), (ts, (128, 256))), 0, 16), w3[...]), 0.0)
    fe[1:17] = even.astype(BF).reshape(16, 16, 256)
    fo[1:17] = odd.astype(BF).reshape(16, 16, 256)
    fm[1:17] = rows_down(odd).astype(BF).reshape(16, 16, 256)
    fp[1:17] = rows_up(even).astype(BF).reshape(16, 16, 256)


def fourth_stage(w4, fe, fo, fm, fp):
    even = jnp.maximum(dot(taps(((fm, FULL), (fe, FULL), (fo, FULL)), 0, 16), w4[...]), 0.0)
    odd = jnp.maximum(dot(taps(((fe, FULL), (fo, FULL), (fp, FULL)), 0, 16), w4[...]), 0.0)
    return jnp.sum(even + odd, axis=0, keepdims=True) * (1.0 / 512)


def pair_feature(loads, w3, w4, sel, wp, w1p, w2p, *maps, between=lambda: None):
    own = [[m.at[v] for m in maps] for v in range(PAIR)]
    for v in range(PAIR):
        tile_stage(loads[v], sel, wp, *own[v][0:2])
        between()
    for chunk in range(4):
        for v in range(PAIR):
            first_stage(chunk, w1p, *own[v][0:4])
            between()
    for v in range(PAIR):
        second_stage(w2p, *own[v][2:6])
        between()
    for v in range(PAIR):
        third_stage(w3, *own[v][4:10])
        between()
    features = []
    for v in range(PAIR):
        features.append(fourth_stage(w4, *own[v][6:10]))
        between()
    return features[0] + features[1]


def net_scratch():
    shapes = [(256, 256), (512, 1024), (1536, 256), (1536, 256)]
    shapes += [(PAIR, 34, 32, 256)] * 2 + [(PAIR, 18, 16, 256)] * 8
    return [pltpu.VMEM(shape, BF) for shape in shapes]


def neighbours():
    s, c = lax.axis_index("span"), lax.axis_index("cnn")
    z, y = c // 4, c % 4
    return (
        (s + 1 - 2 * (s % 2), c),
        ((s + 2) % 8, c),
        ((s + 6) % 8, c),
        (s, (c + 4) % 16),
        (s, (c + 12) % 16),
        (s, z * 4 + (y + 1) % 4),
        (s, z * 4 + (y + 3) % 4),
    )


def seen(d, v):
    def ahead(n):
        return pltpu.roll(v, (128 - n) % 128, 1)

    g = lax.broadcasted_iota(I32, v.shape, 1)
    if d == 0:
        return jnp.where(g % 32 < 16, ahead(16), ahead(112))
    if d == 1:
        return ahead(32)
    if d == 2:
        return ahead(96)
    if d == 3:
        return jnp.where(g % 16 < 12, ahead(4), ahead(116))
    if d == 4:
        return jnp.where(g % 16 >= 4, ahead(124), ahead(12))
    if d == 5:
        return jnp.where(g % 4 < 3, ahead(1), ahead(125))
    return jnp.where(g % 4 >= 1, ahead(127), ahead(3))


def plan_steps(counts, plan):
    extra = counts - 1
    divisor = jnp.maximum(extra, 1)
    bit = []
    for d in range(DIRS):
        rest = jnp.full_like(counts, d)
        for _ in range(d):
            rest = jnp.where(rest >= divisor, rest - divisor, rest)
        bit.append(jnp.left_shift(jnp.ones_like(counts), 1 + rest))
    zero = jnp.zeros_like(counts)
    load = 2 * extra
    passed, taken, number = [zero, zero], [zero, zero], [zero, zero]
    near = zero
    for turn in range(ROUNDS):
        if turn:
            over = (load > GOAL).astype(I32)
            near = over
            for d in range(DIRS):
                near = near | seen(d, over)
        for half, d in ORDER:
            kind = half if d else 0
            open_here = (number[kind] < MOST[kind]) & (load < GOAL)
            there = seen(d, jnp.where(open_here, load + 16 * near, 64))
            wish = load > GOAL
            if turn:
                wish = wish | ((load >= GOAL - 1) & (near > 0) & (there < 16)) | (load - (there & 15) >= 2)
            push = wish & (there < 64) & ((passed[half] & bit[d]) == 0) & (extra > 0)
            gone = push.astype(I32)
            come = seen(BACK[d], gone)
            passed[half] = passed[half] | (gone * bit[d])
            taken[half] = taken[half] | (come << BACK[d])
            number[kind] = number[kind] + come
            load = load - gone + come
            yield
    plan.update(passed=passed, taken=taken, load=load)


def lowest(mask, places):
    place = jnp.int32(-1)
    for i in reversed(range(places)):
        place = jnp.where((mask >> i) & 1 == 1, jnp.int32(i), place)
    return place


def remote(src, dst, send_sem, recv_sem, device):
    return pltpu.make_async_remote_copy(
        src_ref=src, dst_ref=dst, send_sem=send_sem, recv_sem=recv_sem, device_id=device, device_id_type=MESH
    )


def remainder(x, n, bound):
    for _ in range(bound - 1):
        x = jnp.where(x >= n, x - n, x)
    return x


def smooth_steps(total, own_count, edges, bounds, rim_out, rim_in, send_sem, recv_sem):
    s, c = lax.axis_index("span"), lax.axis_index("cnn")
    row = lax.broadcasted_iota(I32, (8, 128), 0)
    lane = lax.broadcasted_iota(I32, (8, 128), 1)
    alive = row < own_count
    smooth = jnp.where(alive, total, 0.0)
    border = 2 * RIM
    weight = jnp.zeros((8, 128), F32)
    for k in range(DEGREE):
        edge = jnp.zeros((8, 128), I32)
        for place in range(SLOTS):
            edge = jnp.where(row == place, edges[k, place], edge)
        inner = border + remainder(edge - border, own_count, SLOTS)
        lookup = jnp.where(edge < border, edge, inner)
        weight = weight + jnp.where(lane == lookup, 1.0 / DEGREE, 0.0)
    share = [weight[:, r : r + 1] for r in range(border + SLOTS)]
    exported_ids = [remainder(bounds[r], own_count, SLOTS) for r in range(RIM)]
    for step in range(ITERS):
        exported = jnp.zeros((8, 128), F32)
        for r in range(RIM):
            line = jnp.sum(jnp.where(row == exported_ids[r], smooth, 0.0), axis=0, keepdims=True)
            exported = jnp.where(row == r, line, exported)
        rim_out[step] = exported
        copies = [
            remote(rim_out.at[step], rim_in.at[step, side], send_sem.at[step, side], recv_sem.at[step, side], other)
            for side, other in enumerate((((s + 1) % 8, c), ((s + 7) % 8, c)))
        ]
        for copy in copies:
            copy.start()
        mean = jnp.zeros((8, 128), F32)
        for r in range(SLOTS):
            mean = mean + share[border + r] * smooth[r : r + 1]
        for copy in copies:
            copy.wait()
        from_below = jnp.where(s > 0, rim_in[step, 0], 0.0)
        from_above = jnp.where(s < 7, rim_in[step, 1], 0.0)
        for r in range(RIM):
            mean = mean + share[r] * from_below[r : r + 1]
            mean = mean + share[RIM + r] * from_above[r : r + 1]
        smooth = jnp.where(alive, 0.5 * smooth + 0.5 * mean, 0.0)
    return smooth


def to_logits(units, head):
    logits = lax.dot_general(
        units, head[...], (((1,), (1,)), ((), ())),
        preferred_element_type=F32, precision=lax.Precision.HIGHEST,
    )
    return jnp.concatenate([logits * (1.0 / VIEWS), jnp.zeros((8, 128 - CLASSES), F32)], axis=1)


def label_kernel(
    views, count, edges, bounds, patch_w, w1_h, w2_h, w3_h, w4_h, head,
    labels, total_out, left_out,
    w1, w2, w3, w4, own0, own_a, own_b, own_c, own_d, early, late, send,
    mine, x_in, c_mine, c_in, back_out, back_in, rim_out, rim_in,
    sel, wp, w1p, w2p, m0, m1, m2, m3, m4, m5, m6, m7, m8, m9,
    own_sem, local_sem, weight_sem, view_send, view_recv,
    x_send, x_recv, c_send, c_recv, b_send, b_recv, r_send, r_recv,
):
    net = (sel, wp, w1p, w2p, m0, m1, m2, m3, m4, m5, m6, m7, m8, m9)
    s, c = lax.axis_index("span"), lax.axis_index("cnn")
    near = neighbours()
    along_x = [((s + o) % 8, c) for o in range(1, 8)]
    along_c = [(s, (c + o) % 16) for o in range(1, 16)]
    barrier = pltpu.get_barrier_semaphore()
    for other in along_x + along_c:
        pl.semaphore_signal(barrier, inc=1, device_id=other, device_id_type=MESH)

    own = ((own_a, own_b), (own_c, own_d))
    copies = [
        pltpu.make_async_copy(
            views.at[pl.ds(1, SLOTS - 1), half * PAIR + j], own[half][j], local_sem.at[half, j]
        )
        for half in range(2)
        for j in range(PAIR)
    ]
    first_copies = [
        pltpu.make_async_copy(src, dst, weight_sem.at[i])
        for i, (src, dst) in enumerate(((w1_h, w1), (w2_h, w2), (w3_h, w3), (w4_h, w4)))
    ]
    first_copies.append(pltpu.make_async_copy(views.at[0], own0, own_sem))
    for copy in copies[:1] + first_copies + copies[1:]:
        copy.start()

    own_count = count[0, 0]
    me = s * 16 + c
    lane = lax.broadcasted_iota(I32, (8, 128), 1)
    mine[...] = jnp.where(lane == me, own_count, 0)
    pl.semaphore_wait(barrier, len(along_x) + len(along_c))
    x_copies = [
        remote(mine, x_in.at[o], x_send.at[o], x_recv.at[o], along_x[o]) for o in range(7)
    ]
    for copy in x_copies:
        copy.start()

    divisor = jnp.maximum(own_count - 1, 1)
    slot = [jnp.int32(1) + lax.rem(jnp.int32(d), divisor) for d in range(DIRS)]
    early_copies, late_copies = [], []

    def pass_on(half, j, directions):
        for d in directions:
            for ch in range(4):
                send[half, j, d, ch] = own[half][j][jnp.clip(slot[d] - 1, 0, SLOTS - 2), ch]
            if half == 0:
                target = early.at[j, BACK[d]]
            elif d == 0:
                target = early.at[j, DIRS]
            else:
                target = late.at[j, BACK[d] - 1]
            copy = remote(
                send.at[half, j, d], target, view_send.at[half, j, d], view_recv.at[half, j, BACK[d]], near[d]
            )
            copy.start()
            (late_copies if half and d else early_copies).append(copy)

    copies[0].wait()
    pass_on(0, 0, range(DIRS))
    for copy in x_copies:
        copy.wait()
    counts = mine[...]
    for o in range(7):
        counts = counts + x_in[o]
    c_mine[...] = counts
    c_copies = [
        remote(c_mine, c_in.at[o], c_send.at[o], c_recv.at[o], along_c[o]) for o in range(15)
    ]
    for copy in c_copies:
        copy.start()
    for copy in copies[1:]:
        copy.wait()
    pass_on(0, 1, range(DIRS))
    pass_on(1, 0, range(1))
    pass_on(1, 1, range(1))
    pass_on(1, 0, range(1, DIRS))
    pass_on(1, 1, range(1, DIRS))
    for copy in first_copies:
        copy.wait()
    prepare(patch_w, w1, w2, *net)
    for copy in c_copies:
        copy.wait()
    for o in range(15):
        counts = counts + c_in[o]
    plan = {}
    steps = plan_steps(counts, plan)

    def go_on():
        for _ in range(2):
            next(steps, None)

    units = []
    for half in range(2):
        loads = [
            lambda ch, first, rows, v=half * PAIR + j: own0[v, ch, pl.ds(first, rows), :]
            for j in range(PAIR)
        ]
        units.append(pair_feature(loads, w3, w4, *net, between=go_on))
    for _ in steps:
        pass

    def here(v):
        return jnp.sum(jnp.where((lane == me)[0:1], v[0:1], 0))

    live = (jnp.left_shift(jnp.int32(1), own_count) - 1) & 254
    kept = [live & ~here(plan["passed"][half]) for half in range(2)]
    got = [here(plan["taken"][half]) for half in range(2)]
    mask = got[0] | ((got[1] & 1) << DIRS)
    mask = mask | ((kept[0] >> 1) << (OWN + 1)) | ((kept[1] >> 1) << (OWN_LATE + 1))
    picks = []
    for _ in range(GOAL):
        pick = lowest(mask, PLACES)
        picks.append(pick)
        last = jnp.where(pick >= 0, jnp.left_shift(jnp.int32(1), jnp.maximum(pick, 0)), 0)
        mask = mask & ~last
    third = picks[-1]
    late_dir = lowest(got[1] & ~1, DIRS)
    has_late = late_dir >= 0
    mask = mask | jnp.where(has_late, last, 0)
    picks[-1] = jnp.where(has_late, PLACES + late_dir, third)

    def at_place(place, j, ch, first, rows):
        pixels = [
            ref[jnp.clip(place - base, 0, most), ch, pl.ds(first, rows), :]
            for ref, base, most in (
                (early.at[j], 0, DIRS),
                (own[0][j], OWN + 1, SLOTS - 2),
                (own[1][j], OWN_LATE + 1, SLOTS - 2),
            )
        ]
        return jnp.where(
            place <= OWN, pixels[0], jnp.where(place <= OWN_LATE, pixels[1], pixels[2])
        )

    for copy in early_copies:
        copy.wait()
    for n in range(GOAL - 1):
        loads = [
            lambda ch, first, rows, j=j, n=n: at_place(picks[n], j, ch, first, rows)
            for j in range(PAIR)
        ]
        units.append(pair_feature(loads, w3, w4, *net))
    for copy in late_copies:
        copy.wait()
    place_late = jnp.clip(late_dir - 1, 0, DIRS - 2)
    loads = [
        lambda ch, first, rows, j=j: jnp.where(
            has_late,
            late[j, place_late, ch, pl.ds(first, rows), :],
            at_place(third, j, ch, first, rows),
        )
        for j in range(PAIR)
    ]
    units.append(pair_feature(loads, w3, w4, *net))

    logits = to_logits(jnp.concatenate(units + [jnp.zeros((8 - len(units), 256), F32)], axis=0), head)
    b_copies = []
    for d in range(DIRS):
        answer = jnp.zeros((8, 128), F32)
        for n, pick in enumerate(picks):
            ours = (pick == d) | (pick == PLACES + d)
            if d == 0:
                ours = ours | (pick == DIRS)
            answer = answer + jnp.where(ours, logits[2 + n : 3 + n], 0.0)
        back_out[d] = answer
        copy = remote(back_out.at[d], back_in.at[BACK[d]], b_send.at[d], b_recv.at[BACK[d]], near[d])
        copy.start()
        b_copies.append(copy)
    row = lax.broadcasted_iota(I32, (8, 128), 0)
    result = jnp.where(row == 0, logits[0:1] + logits[1:2], 0.0)
    for n, pick in enumerate(picks):
        for base in (OWN, OWN_LATE):
            is_own = (pick > base) & (pick < base + SLOTS) & (row == pick - base)
            result = result + jnp.where(is_own, logits[2 + n : 3 + n], 0.0)
    rest0 = (mask >> (OWN + 1)) & 127
    rest1 = (mask >> (OWN_LATE + 1)) & 127
    any_left = jnp.sum((plan["load"][0:1] > GOAL).astype(I32))
    left_out[...] = jnp.where(lane == 0, rest0 | (rest1 << 7), any_left)
    for copy in b_copies:
        copy.wait()
    for d in range(DIRS):
        result = result + jnp.where(row == slot[d], back_in[d], 0.0)
    total_out[...] = result
    smooth = smooth_steps(result, own_count, edges, bounds, rim_out, rim_in, r_send, r_recv)
    labels[...] = smooth[:, 0:CLASSES]


def label(views, count, edges, bounds, patch_w, w1, w2, w3, w4, head):
    dma = pltpu.SemaphoreType.DMA
    pixels = (4, 128, 256)
    tile = (8, 128)
    return pl.pallas_call(
        label_kernel,
        out_shape=(
            jax.ShapeDtypeStruct((SLOTS, CLASSES), F32),
            jax.ShapeDtypeStruct(tile, F32),
            jax.ShapeDtypeStruct(tile, I32),
        ),
        in_specs=[ANY, SMEM, SMEM, SMEM, VMEM, ANY, ANY, ANY, ANY, VMEM],
        out_specs=(VMEM, VMEM, VMEM),
        scratch_shapes=[
            *[pltpu.VMEM(w.shape, BF) for w in (w1, w2, w3, w4)],
            pltpu.VMEM((VIEWS, *pixels), BF),
            *[pltpu.VMEM((SLOTS - 1, *pixels), BF)] * (2 * PAIR),
            pltpu.VMEM((PAIR, DIRS + 1, *pixels), BF),
            pltpu.VMEM((PAIR, DIRS - 1, *pixels), BF),
            pltpu.VMEM((2, PAIR, DIRS, *pixels), BF),
            pltpu.VMEM(tile, I32),
            pltpu.VMEM((7, *tile), I32),
            pltpu.VMEM(tile, I32),
            pltpu.VMEM((15, *tile), I32),
            pltpu.VMEM((DIRS, *tile), F32),
            pltpu.VMEM((DIRS, *tile), F32),
            pltpu.VMEM((ITERS, *tile), F32),
            pltpu.VMEM((ITERS, 2, *tile), F32),
            *net_scratch(),
            dma(()), dma((2, PAIR)), dma((4,)),
            dma((2, PAIR, DIRS)), dma((2, PAIR, DIRS)),
            dma((7,)), dma((7,)), dma((15,)), dma((15,)), dma((DIRS,)), dma((DIRS,)),
            dma((ITERS, 2)), dma((ITERS, 2)),
        ],
        compiler_params=pltpu.CompilerParams(
            collective_id=0, has_side_effects=True, vmem_limit_bytes=58 << 20
        ),
    )(views, count, edges, bounds, patch_w, w1, w2, w3, w4, head)


def rest_kernel(
    left, views, patch_w, w1, w2, w3, w4, head, total,
    total_out, own, pw_v, w1_v, w2_v, w3_v, w4_v, *net_and_sems,
):
    net, sems = net_and_sems[:-1], net_and_sems[-1]
    mask = left[0, 0]
    total_out[...] = total[...]

    @pl.when(mask != 0)
    def _():
        moves = [
            pltpu.make_async_copy(a, b, sems.at[i])
            for i, (a, b) in enumerate(
                ((patch_w, pw_v), (w1, w1_v), (w2, w2_v), (w3, w3_v), (w4, w4_v))
            )
        ]
        for move in moves:
            move.start()
        for move in moves:
            move.wait()
        prepare(pw_v, w1_v, w2_v, *net)

        @pl.loop(0, 2 * (SLOTS - 1))
        def _(i):
            @pl.when((mask >> i) & 1 == 1)
            def _():
                slot, half = 1 + i % (SLOTS - 1), i // (SLOTS - 1)
                move = pltpu.make_async_copy(
                    views.at[slot, pl.ds(half * PAIR, PAIR)], own, sems.at[5]
                )
                move.start()
                move.wait()
                loads = [
                    lambda ch, first, rows, v=j: own[v, ch, pl.ds(first, rows), :]
                    for j in range(PAIR)
                ]
                unit = jnp.broadcast_to(pair_feature(loads, w3_v, w4_v, *net), (8, 256))
                logits = to_logits(unit, head)
                row = lax.broadcasted_iota(I32, (8, 128), 0)
                total_out[...] += jnp.where(row == slot, logits, 0.0)


def rest(left, views, patch_w, w1, w2, w3, w4, head, total):
    pixels = (4, 128, 256)
    return pl.pallas_call(
        rest_kernel,
        out_shape=jax.ShapeDtypeStruct((8, 128), F32),
        in_specs=[SMEM] + [ANY] * 6 + [VMEM] * 2,
        out_specs=VMEM,
        scratch_shapes=[
            pltpu.VMEM((PAIR, *pixels), BF),
            pltpu.VMEM(patch_w.shape, BF),
            pltpu.VMEM(w1.shape, BF),
            pltpu.VMEM(w2.shape, BF),
            pltpu.VMEM(w3.shape, BF),
            pltpu.VMEM(w4.shape, BF),
            *net_scratch(),
            pltpu.SemaphoreType.DMA((6,)),
        ],
        compiler_params=pltpu.CompilerParams(vmem_limit_bytes=58 << 20),
    )(left, views, patch_w, w1, w2, w3, w4, head, total)


def smooth_kernel(total, count, edges, bounds, labels, rim_out, rim_in, send_sem, recv_sem):
    s, c = lax.axis_index("span"), lax.axis_index("cnn")
    barrier = pltpu.get_barrier_semaphore()
    for other in (((s + 1) % 8, c), ((s + 7) % 8, c)):
        pl.semaphore_signal(barrier, inc=1, device_id=other, device_id_type=MESH)
    pl.semaphore_wait(barrier, 2)
    smooth = smooth_steps(
        total[...], count[0, 0], edges, bounds, rim_out, rim_in, send_sem, recv_sem
    )
    labels[...] = smooth[:, 0:CLASSES]


def smoothing(total, count, edges, bounds):
    dma = pltpu.SemaphoreType.DMA
    return pl.pallas_call(
        smooth_kernel,
        out_shape=jax.ShapeDtypeStruct((SLOTS, CLASSES), F32),
        in_specs=[VMEM, SMEM, SMEM, SMEM],
        out_specs=VMEM,
        scratch_shapes=[
            pltpu.VMEM((ITERS, 8, 128), F32),
            pltpu.VMEM((ITERS, 2, 8, 128), F32),
            dma((ITERS, 2)),
            dma((ITERS, 2)),
        ],
        compiler_params=pltpu.CompilerParams(collective_id=1, has_side_effects=True),
    )(total, count, edges, bounds)


def per_device(
    views, live_counts, skeleton_edges, boundary_rows,
    patch_weight, conv_first, conv_second, conv_third, conv_fourth, head_weight,
):
    weights = (
        patch_weight.reshape(64, 128),
        conv_first,
        conv_second,
        conv_third.reshape(1152, 256),
        conv_fourth.reshape(2304, 256),
        head_weight.T,
    )
    edges = skeleton_edges.T
    labels, total, left = label(views, live_counts, edges, boundary_rows, *weights)

    def with_rest():
        return smoothing(rest(left, views, *weights, total), live_counts, edges, boundary_rows)

    return lax.cond(left[0, 1] > 0, with_rest, lambda: labels)


def solution(mesh):
    placed = (
        P(("span", "cnn"), None, None, None, None),
        P("span", "cnn"),
        P(("span", "cnn"), None),
        P(("span", "cnn")),
        P(),
        P(),
        P(),
        P(),
        P(),
        P(),
    )
    return jax.shard_map(
        per_device, mesh=mesh, in_specs=placed, out_specs=P(("span", "cnn"), None), check_vma=False
    )
```

time: 83.6 us -> 57.8 us (0.69)
  Pallas kernels: 73.5 us -> 54 us
  local copies, waits for them, and re-layouts: 8.91 us -> 1.21 us
    pallas_call x3 -> x1, Pallas kernels: 73.5 us -> 54 us  [label(): pl.pallas_call(label_kernel, out_shape=(jax.ShapeDtypeStruct((SLOTS, CLAS...]
    unnamed x25 -> x17, local copies, waits for them, and re-layouts: 8.91 us -> 0.63 us
where the time goes in v2:
time: 57.8 us; the launch traced here: 56.8 us
  Pallas kernels  54 us (93%)
  between operations  1.57 us (3%)
  local copies, waits for them, and re-layouts  1.21 us (2%)
    pallas_call x1, Pallas kernels, label(): pl.pallas_call(label_kernel, out_shape=(jax.ShapeDtypeStruct((SLOTS, CLAS...  54 us

profile of v2, /device:TPU:1, one launch (start us, length us, event | category | flops | bytes accessed | tf_op | source)
XLA Modules:
  0.0 56.8 jit_solution(10029170740122708828)
XLA Ops:
  0.0 0.0 copy-start.3
  0.0 0.0 copy-start.2
  0.0 0.0 copy-start.7
  0.0 0.0 copy-start.5
  0.0 0.0 copy-start
  0.0 0.0 copy-start.1
  0.0 0.0 copy-start.4
  0.0 0.0 copy-start.6
  0.9 54.0 %shard_map.102 = (f32[8,7]{1,0:T(8,128)S(1)}, f32[8,128]{1,0:T(8,128)S(1)}, s32[8,128]{1,0:T(8,128)S(1)}) custom-call(bf16[8,4,4,128,256]{4,3,2,1,0:T(8,128)(2,1)} %views.1, s32[1,1]{1,0:T(1,128)S(6)} %copy.16.count, s32[4,8]{1,0:T(4,128)} %bitcast.14, s32[2]{0:T(128)} %bounds.1, bf16[64,128]{1,0:T(8,128)(2,1)} %bitcast.10, bf16[3,3,128,128]{3,2,1,0:T(8,128)(2,1)} %w1_h.1, ...), custom_call_target="tpu_custom_call" | custom-call | tf_op jit(solution)/shard_map/pallas_call | solution.py:521
  54.9 0.6 %slice.3 = s32[1,1]{1,0:T(1,128)} slice(s32[8,128]{1,0:T(8,128)S(1)} %get-tuple-element.48), slice={[0:1], [1:2]} | slice | bytes 8 | tf_op jit(solution)/shard_map/slice | solution.py:667
  56.1 0.0 copy-done.3
  56.2 0.0 copy-done.2
  56.2 0.0 copy-done.7
  56.2 0.0 copy-done.5
  56.2 0.0 copy-done
  56.2 0.0 copy-done.1
  56.2 0.0 copy-done.4
  56.2 0.0 copy-done.6
  56.2 0.6 %copy.17 = f32[8,7]{1,0:T(8,128)} copy(f32[8,7]{1,0:T(8,128)S(1)} %get-tuple-element.51) | data formatting | bytes 448
  (1 shorter events, 0.0 us)
Async XLA Ops:
  0.0 56.1 %copy-start.3 = (bf16[3,3,128,128]{3,2,1,0:T(8,128)(2,1)S(1)}, bf16[3,3,128,128]{3,2,1,0:T(8,128)(2,1)}, u32[]{:S(2)}) copy-start(bf16[3,3,128,128]{3,2,1,0:T(8,128)(2,1)} %w2_h.1) | copy-start | bytes 884740
  0.0 56.2 %copy-start.2 = (bf16[3,3,128,128]{3,2,1,0:T(8,128)(2,1)S(1)}, bf16[3,3,128,128]{3,2,1,0:T(8,128)(2,1)}, u32[]{:S(2)}) copy-start(bf16[3,3,128,128]{3,2,1,0:T(8,128)(2,1)} %w1_h.1) | copy-start | bytes 884740
  0.0 56.2 %copy-start.7 = (s32[2]{0:T(128)S(1)}, s32[2]{0:T(128)}, u32[]{:S(2)}) copy-start(s32[2]{0:T(128)} %bounds.1) | copy-start | bytes 28
  0.0 56.2 %copy-start.5 = (f32[256,7]{0,1:T(8,128)S(1)}, f32[256,7]{0,1:T(8,128)}, u32[]{:S(2)}) copy-start(f32[256,7]{0,1:T(8,128)} %param.21) | copy-start | bytes 21508
  0.0 56.2 %copy-start = (bf16[3,3,256,256]{3,2,1,0:T(8,128)(2,1)S(1)}, bf16[3,3,256,256]{3,2,1,0:T(8,128)(2,1)}, u32[]{:S(2)}) copy-start(bf16[3,3,256,256]{3,2,1,0:T(8,128)(2,1)} %param.20) | copy-start | bytes 3538948
  0.0 56.2 %copy-start.1 = (bf16[3,3,128,256]{3,2,1,0:T(8,128)(2,1)S(1)}, bf16[3,3,128,256]{3,2,1,0:T(8,128)(2,1)}, u32[]{:S(2)}) copy-start(bf16[3,3,128,256]{3,2,1,0:T(8,128)(2,1)} %param.19) | copy-start | bytes 1769476
  0.0 56.2 %copy-start.4 = (bf16[4,4,4,128]{3,2,1,0:T(4,128)(2,1)S(1)}, bf16[4,4,4,128]{3,2,1,0:T(4,128)(2,1)}, u32[]{:S(2)}) copy-start(bf16[4,4,4,128]{3,2,1,0:T(4,128)(2,1)} %param.16) | copy-start | bytes 49156
  0.0 56.2 %copy-start.6 = (s32[8,4]{0,1:T(4,128)S(1)}, s32[8,4]{0,1:T(4,128)}, u32[]{:S(2)}) copy-start(s32[8,4]{0,1:T(4,128)} %param.14) | copy-start | bytes 388

commit v3 on v2

--- a/solution.py
+++ b/solution.py
@@ -25,9 +25,13 @@
 DIRS = 7
 BACK = (0, 2, 1, 4, 3, 6, 5)
 GOAL = 3
-MOST = (3, 1)
-ROUNDS = 4
-ORDER = [(1, 0), (0, 0)] + [(half, d) for half in range(2) for d in range(1, DIRS)]
+PLAN = (
+    (False, (0,), 0),
+    (False, (1,), 1),
+    (True, (0,), 0),
+    (True, (0, 1), 0),
+    (True, (0, 1), 0),
+)
 OWN = DIRS
 OWN_LATE = OWN + SLOTS - 1
 PLACES = OWN_LATE + SLOTS
@@ -223,28 +227,36 @@
         bit.append(jnp.left_shift(jnp.ones_like(counts), 1 + rest))
     zero = jnp.zeros_like(counts)
     load = 2 * extra
-    passed, taken, number = [zero, zero], [zero, zero], [zero, zero]
+    passed, taken, late = [zero, zero], [zero, zero], zero
     near = zero
-    for turn in range(ROUNDS):
-        if turn:
+    for spread, halves, first in PLAN:
+        if spread:
             over = (load > GOAL).astype(I32)
             near = over
             for d in range(DIRS):
                 near = near | seen(d, over)
-        for half, d in ORDER:
-            kind = half if d else 0
-            open_here = (number[kind] < MOST[kind]) & (load < GOAL)
-            there = seen(d, jnp.where(open_here, load + 16 * near, 64))
-            wish = load > GOAL
-            if turn:
-                wish = wish | ((load >= GOAL - 1) & (near > 0) & (there < 16)) | (load - (there & 15) >= 2)
-            push = wish & (there < 64) & ((passed[half] & bit[d]) == 0) & (extra > 0)
-            gone = push.astype(I32)
-            come = seen(BACK[d], gone)
-            passed[half] = passed[half] | (gone * bit[d])
-            taken[half] = taken[half] | (come << BACK[d])
-            number[kind] = number[kind] + come
-            load = load - gone + come
+        for d in range(first, DIRS):
+            there = seen(d, load + 16 * near + 32 * late)
+            load_there, near_there, late_there = there & 15, there & 16, there & 32
+            gone = [zero, zero]
+            for half in halves if d else (1, 0):
+                wish = load > GOAL
+                if spread:
+                    wish = wish | ((load >= GOAL - 1) & (near > 0) & (near_there == 0))
+                    wish = wish | (load - load_there >= 2)
+                push = wish & (load_there < GOAL) & ((passed[half] & bit[d]) == 0) & (extra > 0)
+                if half and d:
+                    push = push & (late_there == 0)
+                gone[half] = push.astype(I32)
+                passed[half] = passed[half] | (gone[half] * bit[d])
+                load, load_there = load - gone[half], load_there + gone[half]
+            come = seen(BACK[d], gone[0] + 2 * gone[1])
+            came = [come & 1, come >> 1]
+            for half in range(2):
+                taken[half] = taken[half] | (came[half] << BACK[d])
+            if d:
+                late = late | came[1]
+            load = load + came[0] + came[1]
             yield
     plan.update(passed=passed, taken=taken, load=load)
 
@@ -268,47 +280,75 @@
     return x
 
 
-def smooth_steps(total, own_count, edges, bounds, rim_out, rim_in, send_sem, recv_sem):
-    s, c = lax.axis_index("span"), lax.axis_index("cnn")
+def smooth_weights(edges, own_count, exported_below, exported_above):
+    s = lax.axis_index("span")
     row = lax.broadcasted_iota(I32, (8, 128), 0)
     lane = lax.broadcasted_iota(I32, (8, 128), 1)
-    alive = row < own_count
-    smooth = jnp.where(alive, total, 0.0)
-    border = 2 * RIM
-    weight = jnp.zeros((8, 128), F32)
+    rims = [jnp.where(s > 0, SLOTS + e, 127) for e in exported_below]
+    rims += [jnp.where(s < 7, 2 * SLOTS + e, 127) for e in exported_above]
+    weight = jnp.where(lane == row, 0.5, 0.0)
     for k in range(DEGREE):
         edge = jnp.zeros((8, 128), I32)
         for place in range(SLOTS):
             edge = jnp.where(row == place, edges[k, place], edge)
-        inner = border + remainder(edge - border, own_count, SLOTS)
-        lookup = jnp.where(edge < border, edge, inner)
-        weight = weight + jnp.where(lane == lookup, 1.0 / DEGREE, 0.0)
-    share = [weight[:, r : r + 1] for r in range(border + SLOTS)]
-    exported_ids = [remainder(bounds[r], own_count, SLOTS) for r in range(RIM)]
+        target = remainder(edge - 2 * RIM, own_count, SLOTS)
+        for r, rim in enumerate(rims):
+            target = jnp.where(edge == r, rim, target)
+        weight = weight + jnp.where(lane == target, 0.5 / DEGREE, 0.0)
+    return jnp.where(row < own_count, weight, 0.0)
+
+
+def spread_weights(weight, spread):
+    for j in range(3 * SLOTS):
+        spread[j] = jnp.broadcast_to(weight[:, j : j + 1], (8, 128))
+
+
+def smooth_steps(smooth, spread, rim_out, rim_in, send_sem, recv_sem):
+    s, c = lax.axis_index("span"), lax.axis_index("cnn")
     for step in range(ITERS):
-        exported = jnp.zeros((8, 128), F32)
-        for r in range(RIM):
-            line = jnp.sum(jnp.where(row == exported_ids[r], smooth, 0.0), axis=0, keepdims=True)
-            exported = jnp.where(row == r, line, exported)
-        rim_out[step] = exported
+        rim_out[step] = smooth
         copies = [
             remote(rim_out.at[step], rim_in.at[step, side], send_sem.at[step, side], recv_sem.at[step, side], other)
             for side, other in enumerate((((s + 1) % 8, c), ((s + 7) % 8, c)))
         ]
         for copy in copies:
             copy.start()
-        mean = jnp.zeros((8, 128), F32)
+        sums = [jnp.zeros((8, 128), F32) for _ in range(4)]
         for r in range(SLOTS):
-            mean = mean + share[border + r] * smooth[r : r + 1]
-        for copy in copies:
+            sums[r % 4] = sums[r % 4] + spread[r] * rim_out[step, r : r + 1]
+        for side, copy in enumerate(copies):
             copy.wait()
-        from_below = jnp.where(s > 0, rim_in[step, 0], 0.0)
-        from_above = jnp.where(s < 7, rim_in[step, 1], 0.0)
-        for r in range(RIM):
-            mean = mean + share[r] * from_below[r : r + 1]
-            mean = mean + share[RIM + r] * from_above[r : r + 1]
-        smooth = jnp.where(alive, 0.5 * smooth + 0.5 * mean, 0.0)
+            for r in range(SLOTS):
+                term = spread[SLOTS * (side + 1) + r] * rim_in[step, side, r : r + 1]
+                sums[r % 4] = sums[r % 4] + term
+        smooth = (sums[0] + sums[1]) + (sums[2] + sums[3])
     return smooth
+
+
+def apply_weights(spread, own, below, above):
+    sums = [jnp.zeros((8, 128), F32) for _ in range(4)]
+    for i, rows in enumerate((own, below, above)):
+        for r in range(SLOTS):
+            sums[r % 4] = sums[r % 4] + spread[SLOTS * i + r] * rows[r : r + 1]
+    return (sums[0] + sums[1]) + (sums[2] + sums[3])
+
+
+def smooth_at_once(smooth, spread, rim_out, rim_in, send_sem, recv_sem):
+    s, c = lax.axis_index("span"), lax.axis_index("cnn")
+    rim_out[0] = smooth
+    copies = [
+        remote(rim_out.at[0], rim_in.at[i], send_sem.at[i], recv_sem.at[i], ((s + ahead) % 8, c))
+        for i, ahead in enumerate((1, 7, 2, 6))
+    ]
+    for copy in copies:
+        copy.start()
+    for copy in copies:
+        copy.wait()
+    below, above, below2, above2 = [rim_in[i] for i in range(4)]
+    own1 = apply_weights(spread.at[0], smooth, below, above)
+    below1 = apply_weights(spread.at[1], below, below2, smooth)
+    above1 = apply_weights(spread.at[2], above, smooth, above2)
+    return apply_weights(spread.at[0], own1, below1, above1)
 
 
 def to_logits(units, head):
@@ -321,12 +361,12 @@
 
 def label_kernel(
     views, count, edges, bounds, patch_w, w1_h, w2_h, w3_h, w4_h, head,
-    labels, total_out, left_out,
+    labels, more_out,
     w1, w2, w3, w4, own0, own_a, own_b, own_c, own_d, early, late, send,
-    mine, x_in, c_mine, c_in, back_out, back_in, rim_out, rim_in,
+    mine, x_in, c_mine, c_in, back_out, back_in, weight, weight_in, spread, rim_out, rim_in,
     sel, wp, w1p, w2p, m0, m1, m2, m3, m4, m5, m6, m7, m8, m9,
     own_sem, local_sem, weight_sem, view_send, view_recv,
-    x_send, x_recv, c_send, c_recv, b_send, b_recv, r_send, r_recv,
+    x_send, x_recv, c_send, c_recv, w_send, w_recv, b_send, b_recv, r_send, r_recv,
 ):
     net = (sel, wp, w1p, w2p, m0, m1, m2, m3, m4, m5, m6, m7, m8, m9)
     s, c = lax.axis_index("span"), lax.axis_index("cnn")
@@ -350,28 +390,36 @@
         for i, (src, dst) in enumerate(((w1_h, w1), (w2_h, w2), (w3_h, w3), (w4_h, w4)))
     ]
     first_copies.append(pltpu.make_async_copy(views.at[0], own0, own_sem))
-    for copy in copies[:1] + first_copies + copies[1:]:
+    first_copies.insert(2, first_copies.pop())
+    for copy in first_copies + copies:
         copy.start()
 
     own_count = count[0, 0]
     me = s * 16 + c
     lane = lax.broadcasted_iota(I32, (8, 128), 1)
-    mine[...] = jnp.where(lane == me, own_count, 0)
-    pl.semaphore_wait(barrier, len(along_x) + len(along_c))
+    row = lax.broadcasted_iota(I32, (8, 128), 0)
+    exported = [remainder(bounds[r], own_count, SLOTS) for r in range(RIM)]
+    mine[...] = jnp.where(
+        lane == me, jnp.where(row == 0, own_count, jnp.where(row == 1, exported[0], exported[1])), 0
+    )
     x_copies = [
         remote(mine, x_in.at[o], x_send.at[o], x_recv.at[o], along_x[o]) for o in range(7)
     ]
-    for copy in x_copies:
-        copy.start()
+    c_copies = [
+        remote(c_mine, c_in.at[o], c_send.at[o], c_recv.at[o], along_c[o]) for o in range(15)
+    ]
 
     divisor = jnp.maximum(own_count - 1, 1)
     slot = [jnp.int32(1) + lax.rem(jnp.int32(d), divisor) for d in range(DIRS)]
     early_copies, late_copies = [], []
 
-    def pass_on(half, j, directions):
+    def fill(half, j, directions):
         for d in directions:
             for ch in range(4):
                 send[half, j, d, ch] = own[half][j][jnp.clip(slot[d] - 1, 0, SLOTS - 2), ch]
+
+    def pass_on(half, j, directions):
+        for d in directions:
             if half == 0:
                 target = early.at[j, BACK[d]]
             elif d == 0:
@@ -384,39 +432,90 @@
             copy.start()
             (late_copies if half and d else early_copies).append(copy)
 
-    copies[0].wait()
-    pass_on(0, 0, range(DIRS))
-    for copy in x_copies:
-        copy.wait()
-    counts = mine[...]
-    for o in range(7):
-        counts = counts + x_in[o]
-    c_mine[...] = counts
-    c_copies = [
-        remote(c_mine, c_in.at[o], c_send.at[o], c_recv.at[o], along_c[o]) for o in range(15)
+    plan = {}
+
+    def enter():
+        pl.semaphore_wait(barrier, len(along_x) + len(along_c))
+        for copy in x_copies:
+            copy.start()
+
+    def begin():
+        copies[0].wait()
+        fill(0, 0, range(DIRS))
+
+    def counts_on():
+        for copy in x_copies:
+            copy.wait()
+        counts = mine[...]
+        for o in range(7):
+            counts = counts + x_in[o]
+        c_mine[...] = counts
+        for copy in c_copies:
+            copy.start()
+        pass_on(0, 0, range(DIRS))
+
+    def second_views():
+        copies[1].wait()
+        fill(0, 1, range(DIRS))
+        pass_on(0, 1, range(DIRS))
+
+    def second_halves():
+        for j in range(PAIR):
+            copies[PAIR + j].wait()
+            fill(1, j, range(1))
+            pass_on(1, j, range(1))
+
+    def late_views(j):
+        fill(1, j, range(1, DIRS))
+        pass_on(1, j, range(1, DIRS))
+
+    def weights_here():
+        for copy in first_copies[3:]:
+            copy.wait()
+
+    w_copies = [
+        remote(weight, weight_in.at[i], w_send.at[i], w_recv.at[i], along_x[ahead - 1])
+        for i, ahead in enumerate((1, 7))
     ]
-    for copy in c_copies:
-        copy.start()
-    for copy in copies[1:]:
-        copy.wait()
-    pass_on(0, 1, range(DIRS))
-    pass_on(1, 0, range(1))
-    pass_on(1, 1, range(1))
-    pass_on(1, 0, range(1, DIRS))
-    pass_on(1, 1, range(1, DIRS))
-    for copy in first_copies:
+
+    def work():
+        yield
+        begin()
+        counts_on()
+        second_views()
+        for _ in range(8):
+            yield
+        weights_here()
+        second_halves()
+        late_views(0)
+        late_views(1)
+
+    def planning():
+        for copy in c_copies:
+            copy.wait()
+        counts = c_mine[...]
+        for o in range(15):
+            counts = counts + c_in[o]
+        below = jnp.where(lane == lax.rem(me + 112, 128), counts, 0)
+        above = jnp.where(lane == lax.rem(me + 16, 128), counts, 0)
+        rims = [[jnp.sum(v[1 + r : 2 + r]) for r in range(RIM)] for v in (below, above)]
+        weight[...] = smooth_weights(edges, own_count, *rims)
+        for copy in w_copies:
+            copy.start()
+        for n, _ in enumerate(plan_steps(jnp.broadcast_to(counts[0:1], (8, 128)), plan)):
+            if n % 3 == 2:
+                yield
+
+    def spreading():
+        for i, tile in enumerate((weight, weight_in.at[0], weight_in.at[1])):
+            spread_weights(tile[...], spread.at[i])
+            yield
+
+    enter()
+    for copy in first_copies[:2]:
         copy.wait()
     prepare(patch_w, w1, w2, *net)
-    for copy in c_copies:
-        copy.wait()
-    for o in range(15):
-        counts = counts + c_in[o]
-    plan = {}
-    steps = plan_steps(counts, plan)
-
-    def go_on():
-        for _ in range(2):
-            next(steps, None)
+    first_copies[2].wait()
 
     units = []
     for half in range(2):
@@ -424,9 +523,10 @@
             lambda ch, first, rows, v=half * PAIR + j: own0[v, ch, pl.ds(first, rows), :]
             for j in range(PAIR)
         ]
-        units.append(pair_feature(loads, w3, w4, *net, between=go_on))
-    for _ in steps:
-        pass
+        task = (work, planning)[half]()
+        units.append(pair_feature(loads, w3, w4, *net, between=lambda task=task: next(task, None)))
+        for _ in task:
+            pass
 
     def here(v):
         return jnp.sum(jnp.where((lane == me)[0:1], v[0:1], 0))
@@ -469,7 +569,7 @@
             for j in range(PAIR)
         ]
         units.append(pair_feature(loads, w3, w4, *net))
-    for copy in late_copies:
+    for copy in late_copies + w_copies:
         copy.wait()
     place_late = jnp.clip(late_dir - 1, 0, DIRS - 2)
     loads = [
@@ -480,7 +580,8 @@
         )
         for j in range(PAIR)
     ]
-    units.append(pair_feature(loads, w3, w4, *net))
+    task = spreading()
+    units.append(pair_feature(loads, w3, w4, *net, between=lambda: next(task, None)))
 
     logits = to_logits(jnp.concatenate(units + [jnp.zeros((8 - len(units), 256), F32)], axis=0), head)
     b_copies = []
@@ -495,7 +596,6 @@
         copy = remote(back_out.at[d], back_in.at[BACK[d]], b_send.at[d], b_recv.at[BACK[d]], near[d])
         copy.start()
         b_copies.append(copy)
-    row = lax.broadcasted_iota(I32, (8, 128), 0)
     result = jnp.where(row == 0, logits[0:1] + logits[1:2], 0.0)
     for n, pick in enumerate(picks):
         for base in (OWN, OWN_LATE):
@@ -504,13 +604,15 @@
     rest0 = (mask >> (OWN + 1)) & 127
     rest1 = (mask >> (OWN_LATE + 1)) & 127
     any_left = jnp.sum((plan["load"][0:1] > GOAL).astype(I32))
-    left_out[...] = jnp.where(lane == 0, rest0 | (rest1 << 7), any_left)
+    more_out[2] = jnp.where(lane == 0, rest0 | (rest1 << 7), any_left).astype(F32)
+    more_out[1] = weight[...]
     for copy in b_copies:
         copy.wait()
     for d in range(DIRS):
         result = result + jnp.where(row == slot[d], back_in[d], 0.0)
-    total_out[...] = result
-    smooth = smooth_steps(result, own_count, edges, bounds, rim_out, rim_in, r_send, r_recv)
+    result = jnp.where(row < own_count, result, 0.0)
+    more_out[0] = result
+    smooth = smooth_at_once(result, spread, rim_out, rim_in, r_send, r_recv)
     labels[...] = smooth[:, 0:CLASSES]
 
 
@@ -522,11 +624,10 @@
         label_kernel,
         out_shape=(
             jax.ShapeDtypeStruct((SLOTS, CLASSES), F32),
-            jax.ShapeDtypeStruct(tile, F32),
-            jax.ShapeDtypeStruct(tile, I32),
+            jax.ShapeDtypeStruct((3, *tile), F32),
         ),
         in_specs=[ANY, SMEM, SMEM, SMEM, VMEM, ANY, ANY, ANY, ANY, VMEM],
-        out_specs=(VMEM, VMEM, VMEM),
+        out_specs=(VMEM, VMEM),
         scratch_shapes=[
             *[pltpu.VMEM(w.shape, BF) for w in (w1, w2, w3, w4)],
             pltpu.VMEM((VIEWS, *pixels), BF),
@@ -540,13 +641,16 @@
             pltpu.VMEM((15, *tile), I32),
             pltpu.VMEM((DIRS, *tile), F32),
             pltpu.VMEM((DIRS, *tile), F32),
-            pltpu.VMEM((ITERS, *tile), F32),
-            pltpu.VMEM((ITERS, 2, *tile), F32),
+            pltpu.VMEM(tile, F32),
+            pltpu.VMEM((2, *tile), F32),
+            pltpu.VMEM((3, 3 * SLOTS, *tile), F32),
+            pltpu.VMEM((1, *tile), F32),
+            pltpu.VMEM((4, *tile), F32),
             *net_scratch(),
             dma(()), dma((2, PAIR)), dma((4,)),
             dma((2, PAIR, DIRS)), dma((2, PAIR, DIRS)),
-            dma((7,)), dma((7,)), dma((15,)), dma((15,)), dma((DIRS,)), dma((DIRS,)),
-            dma((ITERS, 2)), dma((ITERS, 2)),
+            dma((7,)), dma((7,)), dma((15,)), dma((15,)), dma((2,)), dma((2,)),
+            dma((DIRS,)), dma((DIRS,)), dma((4,)), dma((4,)),
         ],
         compiler_params=pltpu.CompilerParams(
             collective_id=0, has_side_effects=True, vmem_limit_bytes=58 << 20
@@ -559,7 +663,7 @@
     total_out, own, pw_v, w1_v, w2_v, w3_v, w4_v, *net_and_sems,
 ):
     net, sems = net_and_sems[:-1], net_and_sems[-1]
-    mask = left[0, 0]
+    mask = left[0, 0].astype(I32)
     total_out[...] = total[...]
 
     @pl.when(mask != 0)
@@ -617,33 +721,33 @@
     )(left, views, patch_w, w1, w2, w3, w4, head, total)
 
 
-def smooth_kernel(total, count, edges, bounds, labels, rim_out, rim_in, send_sem, recv_sem):
+def smooth_kernel(total, weight, labels, spread, rim_out, rim_in, send_sem, recv_sem):
     s, c = lax.axis_index("span"), lax.axis_index("cnn")
     barrier = pltpu.get_barrier_semaphore()
     for other in (((s + 1) % 8, c), ((s + 7) % 8, c)):
         pl.semaphore_signal(barrier, inc=1, device_id=other, device_id_type=MESH)
+    spread_weights(weight[...], spread)
     pl.semaphore_wait(barrier, 2)
-    smooth = smooth_steps(
-        total[...], count[0, 0], edges, bounds, rim_out, rim_in, send_sem, recv_sem
-    )
+    smooth = smooth_steps(total[...], spread, rim_out, rim_in, send_sem, recv_sem)
     labels[...] = smooth[:, 0:CLASSES]
 
 
-def smoothing(total, count, edges, bounds):
+def smoothing(total, weight):
     dma = pltpu.SemaphoreType.DMA
     return pl.pallas_call(
         smooth_kernel,
         out_shape=jax.ShapeDtypeStruct((SLOTS, CLASSES), F32),
-        in_specs=[VMEM, SMEM, SMEM, SMEM],
+        in_specs=[VMEM, VMEM],
         out_specs=VMEM,
         scratch_shapes=[
+            pltpu.VMEM((3 * SLOTS, 8, 128), F32),
             pltpu.VMEM((ITERS, 8, 128), F32),
             pltpu.VMEM((ITERS, 2, 8, 128), F32),
             dma((ITERS, 2)),
             dma((ITERS, 2)),
         ],
         compiler_params=pltpu.CompilerParams(collective_id=1, has_side_effects=True),
-    )(total, count, edges, bounds)
+    )(total, weight)
 
 
 def per_device(
@@ -658,13 +762,12 @@
         conv_fourth.reshape(2304, 256),
         head_weight.T,
     )
-    edges = skeleton_edges.T
-    labels, total, left = label(views, live_counts, edges, boundary_rows, *weights)
+    labels, more = label(views, live_counts, skeleton_edges.T, boundary_rows, *weights)
 
     def with_rest():
-        return smoothing(rest(left, views, *weights, total), live_counts, edges, boundary_rows)
-
-    return lax.cond(left[0, 1] > 0, with_rest, lambda: labels)
+        return smoothing(rest(more[2], views, *weights, more[0]), more[1])
+
+    return lax.cond(more[2, 0, 1] > 0, with_rest, lambda: labels)
 
 
 def solution(mesh):

time: 57.8 us -> 54.1 us (0.936); the launches traced: 56.8 us -> 54 us
  Pallas kernels: 54 us -> 51.2 us
    pallas_call x1, Pallas kernels: 54 us -> 51.2 us  [label(): pl.pallas_call(label_kernel, out_shape=(jax.ShapeDtypeStruct((SLOTS, CLAS...]
where the time goes in v3:
time: 54.1 us; the launch traced here: 54 us
  Pallas kernels  51.2 us (95%)
  between operations  1.54 us (3%)
  local copies, waits for them, and re-layouts  1.2 us (2%)
    pallas_call x1, Pallas kernels, label(): pl.pallas_call(label_kernel, out_shape=(jax.ShapeDtypeStruct((SLOTS, CLAS...  51.2 us

profile of v3, /device:TPU:1, one launch (start us, length us, event | category | flops | bytes accessed | tf_op | source)
XLA Modules:
  0.0 54.0 jit_solution(1583316733565567715)
XLA Ops:
  0.0 0.0 copy-start.3
  0.0 0.0 copy-start.2
  0.0 0.0 copy-start.5
  0.0 0.0 copy-start
  0.0 0.0 copy-start.1
  0.0 0.0 copy-start.4
  0.8 51.2 %shard_map.102 = (f32[8,7]{1,0:T(8,128)S(1)}, f32[3,8,128]{2,1,0:T(8,128)S(1)}) custom-call(bf16[8,4,4,128,256]{4,3,2,1,0:T(8,128)(2,1)} %views.1, s32[1,1]{1,0:T(1,128)S(6)} %copy.16.count, s32[4,8]{1,0:T(4,128)} %bitcast.20, s32[2]{0:T(128)} %bounds.1, bf16[64,128]{1,0:T(8,128)(2,1)} %bitcast.16, bf16[3,3,128,128]{3,2,1,0:T(8,128)(2,1)} %w1_h.1, ...), custom_call_target="tpu_custom_call" | custom-call | tf_op jit(solution)/shard_map/pallas_call | solution.py:623
  52.1 0.6 %slice.12 = f32[1,1,1]{2,1,0:T(1,128)} slice(f32[3,8,128]{2,1,0:T(8,128)S(1)} %get-tuple-element.35), slice={[2:3], [0:1], [1:2]} | slice | bytes 8 | tf_op jit(solution)/shard_map/slice | solution.py:770
  53.3 0.0 copy-done.3
  53.3 0.0 copy-done.2
  53.3 0.0 copy-done.5
  53.3 0.0 copy-done
  53.3 0.0 copy-done.1
  53.3 0.0 copy-done.4
  53.4 0.6 %copy.17 = f32[8,7]{1,0:T(8,128)} copy(f32[8,7]{1,0:T(8,128)S(1)} %get-tuple-element.37) | data formatting | bytes 448
  (1 shorter events, 0.0 us)
Async XLA Ops:
  0.0 53.3 %copy-start.3 = (bf16[3,3,128,128]{3,2,1,0:T(8,128)(2,1)S(1)}, bf16[3,3,128,128]{3,2,1,0:T(8,128)(2,1)}, u32[]{:S(2)}) copy-start(bf16[3,3,128,128]{3,2,1,0:T(8,128)(2,1)} %w2_h.1) | copy-start | bytes 884740
  0.0 53.3 %copy-start.2 = (bf16[3,3,128,128]{3,2,1,0:T(8,128)(2,1)S(1)}, bf16[3,3,128,128]{3,2,1,0:T(8,128)(2,1)}, u32[]{:S(2)}) copy-start(bf16[3,3,128,128]{3,2,1,0:T(8,128)(2,1)} %w1_h.1) | copy-start | bytes 884740
  0.0 53.3 %copy-start.5 = (f32[256,7]{0,1:T(8,128)S(1)}, f32[256,7]{0,1:T(8,128)}, u32[]{:S(2)}) copy-start(f32[256,7]{0,1:T(8,128)} %param.21) | copy-start | bytes 21508
  0.0 53.3 %copy-start = (bf16[3,3,256,256]{3,2,1,0:T(8,128)(2,1)S(1)}, bf16[3,3,256,256]{3,2,1,0:T(8,128)(2,1)}, u32[]{:S(2)}) copy-start(bf16[3,3,256,256]{3,2,1,0:T(8,128)(2,1)} %param.20) | copy-start | bytes 3538948
  0.0 53.3 %copy-start.1 = (bf16[3,3,128,256]{3,2,1,0:T(8,128)(2,1)S(1)}, bf16[3,3,128,256]{3,2,1,0:T(8,128)(2,1)}, u32[]{:S(2)}) copy-start(bf16[3,3,128,256]{3,2,1,0:T(8,128)(2,1)} %param.19) | copy-start | bytes 1769476
  0.0 53.3 %copy-start.4 = (bf16[4,4,4,128]{3,2,1,0:T(4,128)(2,1)S(1)}, bf16[4,4,4,128]{3,2,1,0:T(4,128)(2,1)}, u32[]{:S(2)}) copy-start(bf16[4,4,4,128]{3,2,1,0:T(4,128)(2,1)} %param.16) | copy-start | bytes 49156
